TPU v7x, 32 devices: a whole 2x2x4 slice. The times are simulated.
32 devices in a mesh: seq: 8 (over z, y), head: 4 (over x, core).
Axes of the slice: x: 2, y: 2, z: 4, core: 2. Of those that a mesh axis runs over, the one named last changes fastest.
Arguments:
- x_heads: bfloat16 [4096, 32768], P(('head', 'seq')), may hold values from -6 to 6
- b_proj: bfloat16 [32768, 128], P(('seq', 'head')), may hold values from -0.5 to 0.5
- c_proj: bfloat16 [32768, 128], P(('seq', 'head')), may hold values from -6 to 6
- log_gate: float32 [64, 32768], P('head', 'seq'), may hold values from -3 to 0, as said below
- step_size: float32 [64, 32768], P('head', 'seq'), may hold values from 0.003 to 0.03
- level_weight: float32 [64, 8, 32768], P('head', None, 'seq'), may hold values from 0.25 to 4
- skip: float32 [64], P('head'), may hold values from 0.5 to 1.5
Outputs:
- y_heads: bfloat16 [4096, 32768], P(('head', 'seq'))
Inputs may be any that keep to these rules, and one draw needn't show every extreme that they name: log_gate holds no positive values.
All inputs are finite; a program needn't handle non-finite values.
Results may differ from a plain program's by a relative error of at most 0.0064.
Values may be sent and summed in bfloat16 or wider, within the bound.
No kernel may reach another device: no remote copies, remote signals or barrier semaphores. Data moves between devices by JAX's collectives and lax.ppermute only.
A program may use at most 192 MiB of HBM per device.

v0:
```python
import functools
import math

import jax
import jax.numpy as jnp
from jax import lax
from jax.experimental import pallas as pl
from jax.experimental.pallas import tpu as pltpu
from jax.sharding import PartitionSpec as P

P_SIZE = 64
N = 128
Q = 256
HALF = Q // 2
CORES = 2
NEVER = -1e30
VMEM_LIMIT = 60 * 1024 * 1024

f32 = jnp.float32
bf16 = jnp.bfloat16


def dot(a, b):
    return lax.dot_general(a, b, (((1,), (0,)), ((), ())), preferred_element_type=f32)


def exact_parts(value):
    high = value.astype(bf16)
    rest = value - high.astype(f32)
    middle = rest.astype(bf16)
    low = (rest - middle.astype(f32)).astype(bf16)
    return high, middle, low


def gates_kernel(heads, levels, padded, gates_ref, weight_ref, cum_ref, offset_ref, half_ref, decay_ref,
                 merge_ref, log_scratch):
    shards, _, span_rows, _ = gates_ref.shape
    spans = shards * span_rows
    upper = (
        lax.broadcasted_iota(jnp.int32, (Q, Q), 0) <= lax.broadcasted_iota(jnp.int32, (Q, Q), 1)
    ).astype(f32).astype(bf16)
    chunk = min(spans, 64)
    for head in range(heads):
        for shard in range(shards):
            rows = pl.ds(shard * span_rows, span_rows)
            gate = gates_ref[shard, 2 * head]
            step = gates_ref[shard, 2 * head + 1]
            high, middle, low = exact_parts(gate)
            cumulative = dot(high, upper) + dot(middle, upper) + dot(low, upper)
            span_log = cumulative[:, Q - 1 :]
            cum_ref[head, rows, :] = cumulative
            offset_ref[head, rows, :] = cumulative - jnp.log(step)
            half_log = cumulative[:, HALF - 1 : HALF]
            weight_ref[head, rows, :HALF] = jnp.exp(half_log - cumulative[:, :HALF]) * step[:, :HALF]
            weight_ref[head, rows, HALF:] = jnp.exp(span_log - cumulative[:, HALF:]) * step[:, HALF:]
            half_ref[head, rows, :] = jnp.broadcast_to(jnp.exp(span_log - half_log), (span_rows, N))
            log_scratch[rows, :] = jnp.broadcast_to(span_log, (span_rows, N))
        high, middle, low = exact_parts(log_scratch[...])

        def some_spans(at, carry):
            first = at * chunk
            size = (chunk * padded, spans)
            row = lax.broadcasted_iota(jnp.int32, size, 0)
            span = first + row // padded
            level = row % padded
            other = lax.broadcasted_iota(jnp.int32, size, 1)
            out_rows = pl.ds(pl.multiple_of(first * padded, chunk * padded), chunk * padded)
            bit = jnp.maximum(level - 1, 0)
            before = (other >= (span >> bit) << bit) & (other < span)
            before = before.astype(f32).astype(bf16)
            decay = dot(before, high) + dot(before, middle) + dot(before, low)
            has_bit = ((span >> bit) & 1)[:, :1] == 1
            decay_ref[head, out_rows, :] = jnp.where(has_bit, decay, NEVER)
            right = (other > span - (1 << bit)) & (other <= span)
            right = right.astype(f32).astype(bf16)
            merge_ref[head, out_rows, :] = jnp.exp(
                dot(right, high) + dot(right, middle) + dot(right, low)
            )
            return carry

        lax.fori_loop(0, spans // chunk, some_spans, 0)


def pick_set(step, starts, values):
    value = values[0]
    for start, other in zip(starts[1:], values[1:]):
        value = jnp.where(step >= start, other, value)
    return value


def pick(core, step, starts, pairs, local, group):
    half = group // CORES
    rows = slice(local % half * Q, (local % half + 1) * Q)
    mine = core == local // half
    return pick_set(step, starts, [jnp.where(mine, my_ref[rows, :], other_ref[rows, :]) for my_ref, other_ref in pairs])


def scaled(value, rows, width):
    parts = [value[head * width : (head + 1) * width] * row for head, row in enumerate(rows)]
    return jnp.concatenate(parts, axis=0) if len(parts) > 1 else parts[0]


def merge_blocks(left, right, merge_ref, row, width):
    return scaled(left, [merge_ref[head, row : row + 1, :] for head in range(merge_ref.shape[0])], width) + right


def states_kernel(heads, width, group, padded, starts, groups_ref, core_ref, x_ref, weight_ref, half_ref, merge_ref,
                  *refs):
    *key_refs, low_ref, total_ref = refs
    pairs = list(zip(key_refs[::2], key_refs[1::2]))
    kept = {}
    for local in range(group):
        columns = slice(local * Q, (local + 1) * Q)
        weights = [weight_ref[head, local : local + 1, :] for head in range(heads)]
        weighted = scaled(x_ref[:, columns].astype(f32), weights, width).astype(bf16)
        keys = pick(core_ref[0], pl.program_id(0), starts, pairs, local, group)
        first = dot(weighted[:, :HALF], keys[:HALF])
        low_ref[group + local] = first.astype(bf16)
        halves = [half_ref[head, local : local + 1, :] for head in range(heads)]
        state = scaled(first, halves, width) + dot(weighted[:, HALF:], keys[HALF:])
        bit = 0
        while local >> bit & 1:
            state = merge_blocks(kept[bit], state, merge_ref, local * padded + bit + 1, width)
            bit += 1
        kept[bit] = state
        low_ref[local] = state.astype(bf16)
    total_ref[...] = state


def tree_kernel(width, group, padded, groups_ref, merge_ref, *refs):
    *total_refs, high_ref, order_ref = refs
    steps = order_ref.shape[0]
    low_bits = group.bit_length() - 1
    at = 0
    for total_ref in total_refs:
        for slot in range(total_ref.shape[0]):
            order_ref[groups_ref[at]] = total_ref[slot]
            at += 1
    kept = {}
    for step in range(steps):
        state = order_ref[step]
        bit = 0
        while step >> bit & 1:
            row = step * padded + low_bits + bit + 1
            state = merge_blocks(kept[bit], state, merge_ref, row, width)
            bit += 1
        kept[bit] = state
        high_ref[step] = state.astype(bf16)


def outputs_kernel(heads, width, group, bits, padded, starts, groups_ref, core_ref, skip_ref, x_ref, high_ref,
                   cum_ref, offset_ref, decay_ref, level_ref, *refs):
    *set_refs, out_ref, query_ref, score_ref, sum_ref, factor_ref, own_ref, mixing_ref = refs
    set_refs = [set_refs[5 * at : 5 * at + 5] for at in range(len(starts))]
    key_pairs = [refs[0:2] for refs in set_refs]
    query_pairs = [refs[2:4] for refs in set_refs]
    low_refs = [refs[4] for refs in set_refs]
    at = pl.program_id(0)
    step = groups_ref[at]
    low_bits = group.bit_length() - 1
    levels = bits + 1
    causal = lax.broadcasted_iota(jnp.int32, (HALF, HALF), 0) <= lax.broadcasted_iota(
        jnp.int32, (HALF, HALF), 1
    )
    halves = slice(0, HALF), slice(HALF, Q)
    spans = [slice(local * Q, (local + 1) * Q) for local in range(group)]
    head_rows = [slice(head * width, (head + 1) * width) for head in range(heads)]
    high_slots = [
        jnp.maximum((step >> (bit - low_bits) << (bit - low_bits)) - 1, 0) for bit in range(low_bits, bits)
    ]
    offsets = [jnp.transpose(offset_ref[head]) for head in range(heads)]

    def low_state(slot):
        return pick_set(at, starts, [low_ref[slot] for low_ref in low_refs])

    for local, columns in enumerate(spans):
        query_ref[:, columns] = jnp.transpose(pick(core_ref[0], at, starts, query_pairs, local, group))
    right = lax.broadcasted_iota(jnp.int32, (1, Q), 1) >= HALF
    for local, columns in enumerate(spans):
        weights = level_ref[0, :, columns].astype(f32)
        for head in range(heads):
            cumulative = cum_ref[head, local : local + 1, :]
            weight = weights[head * levels : (head + 1) * levels]
            decay = decay_ref[head, local * padded : local * padded + levels, :]
            decay = jnp.concatenate([decay] * (Q // N), axis=1)
            factor_ref[head, :levels, columns] = weight * jnp.exp(cumulative + decay)
            own = cumulative + jnp.log(weight[:1])
            own_ref[head, :1, columns] = own
            across = jnp.exp(own - cumulative[:, HALF - 1 : HALF])
            factor_ref[head, :1, columns] = jnp.where(right, across, 0.0)

    for local, columns in enumerate(spans):
        keys = pick(core_ref[0], at, starts, key_pairs, local, group)
        active = [bit for bit in range(bits) if bit >= low_bits or local >> bit & 1]
        states = [low_state(group + local)]
        for bit in active:
            if bit < low_bits:
                states.append(low_state(((local >> bit) << bit) - 1))
            else:
                states.append(high_ref[high_slots[bit - low_bits]])
        result = dot(jnp.concatenate([keys] + states, axis=0), query_ref[:, columns])
        for half in halves:
            score_ref[local, half] = jnp.where(causal, result[half, half], 0.0)
        for head, rows in enumerate(head_rows):
            total = None
            for place, row in enumerate([0] + [bit + 1 for bit in active]):
                first_row = Q + place * heads * width + rows.start
                term = result[first_row : first_row + width] * factor_ref[head, row : row + 1, columns]
                total = term if total is None else total + term
            sum_ref[rows, columns] = total

    for local, columns in enumerate(spans):
        for head in range(heads):
            own = own_ref[head, :1, columns]
            column = offsets[head][:, local : local + 1]
            for half in halves:
                gaps = jnp.minimum(own[:, half] - column[half], 64.0)
                mixing_ref[local, head, half] = (score_ref[local, half] * jnp.exp(gaps)).astype(bf16)

    for local, columns in enumerate(spans):
        for head, rows in enumerate(head_rows):
            for half in halves:
                here = slice(columns.start + half.start, columns.start + half.stop)
                values = x_ref[rows, here]
                result = dot(values, mixing_ref[local, head, half]) + sum_ref[rows, here]
                out_ref[rows, here] = (result + skip_ref[head] * values.astype(f32)).astype(bf16)


def exchange(value, axis, distance):
    pairs = [(place, place ^ distance) for place in range(lax.axis_size(axis))]
    return lax.ppermute(value, axis, pairs)


def along_z(own):
    pieces = [own]
    for distance in range(1, lax.axis_size("z")):
        low = distance & -distance
        pieces.append(exchange(pieces[distance ^ low], "z", low))
    return pieces[1:]


def places():
    both = [(y, x) for y in range(lax.axis_size("y")) for x in range(lax.axis_size("x"))]
    return sorted(both, key=lambda place: ((place[0] > 0) + (place[1] > 0), place))


def straight(piece):
    near = {(0, 0): piece}
    for y, x in places():
        if (y > 0) != (x > 0):
            near[y, x] = exchange(piece, "x", x) if x else exchange(piece, "y", y)
    return near


def diagonal(near, by_x, by_y, cuts=None):
    far = {}
    cuts = [] if cuts is None else cuts
    for y, x in places():
        if y and x:
            parts = []
            if by_x is not None:
                cuts.append(near[0, x][by_x])
                parts.append(exchange(cuts[-1], "y", y))
            if by_y is not None:
                cuts.append(near[y, 0][by_y])
                parts.append(exchange(cuts[-1], "x", x))
            far[y, x] = parts
    return far


def join(parts):
    return jnp.concatenate(parts, axis=0) if len(parts) > 1 else parts[0]


def with_core(piece):
    return piece, exchange(piece, "core", 1)


def after(value, *others):
    return lax.optimization_barrier((value, *others))[0]


def on_device(x_heads, b_proj, c_proj, log_gate, step_size, level_weight, skip):
    rows, tokens = x_heads.shape
    head_count, tok_dev = log_gate.shape
    levels = level_weight.shape[1]
    bits = levels - 1
    shards = lax.axis_size(("z", "y"))
    span_rows = tok_dev // Q
    spans = tokens // Q
    heads = max(rows // P_SIZE, 1)
    width = rows // heads
    sharing = P_SIZE // width
    block = b_proj.shape[0]
    group = CORES * block // Q
    padded = -(-levels // 8) * 8
    steps = spans // group
    per_shard = span_rows // group

    def to_owners(value):
        value = jnp.repeat(value, sharing, axis=0) if sharing > 1 else value
        value = value.reshape((shards, heads) + value.shape[1:])
        return value.reshape((shards, -1) + value.shape[3:])

    first_head = lax.axis_index(("z", "y")) * rows // P_SIZE
    own_skip = lax.dynamic_slice_in_dim(skip, first_head, heads, 0)
    core = lax.axis_index("core").astype(jnp.int32).reshape(1)

    def group_ids(place, z=None):
        z = lax.axis_index("z") ^ jnp.arange(1, lax.axis_size("z")) if z is None else z
        y = lax.axis_index("y") ^ place[0]
        x = lax.axis_index("x") ^ place[1]
        return ((z * lax.axis_size("y") + y) * lax.axis_size("x") + x).astype(jnp.int32)

    params = pltpu.CompilerParams(vmem_limit_bytes=VMEM_LIMIT)
    key_near = straight(b_proj)
    key_line = along_z(b_proj)
    gates = jnp.stack(
        [log_gate.reshape(head_count, span_rows, Q), step_size.reshape(head_count, span_rows, Q)], axis=1
    )
    gates = lax.all_to_all(to_owners(gates), ("z", "y"), split_axis=0, concat_axis=0, tiled=True)
    query_near = straight(c_proj)
    crossed = [near[place] for near in (key_near, query_near) for place in places() if place in near and any(place)]
    everything = slice(None)
    key_near.update({place: join(parts) for place, parts in diagonal(key_near, everything, None).items()})
    query_near.update({place: join(parts) for place, parts in diagonal(query_near, None, everything).items()})
    keys_here = with_core(join([key_near[place] for place in places()]))

    params = pltpu.CompilerParams(vmem_limit_bytes=VMEM_LIMIT)
    weight, cumulative, offset, half, decay, merge = pl.pallas_call(
        functools.partial(gates_kernel, heads, levels, padded),
        out_shape=[jax.ShapeDtypeStruct((heads, spans, Q), f32)] * 3
        + [jax.ShapeDtypeStruct((heads, spans, N), f32)]
        + [jax.ShapeDtypeStruct((heads, spans * padded, N), f32)] * 2,
        scratch_shapes=[pltpu.VMEM((spans, N), f32)],
        compiler_params=params,
        name="gates",
    )(gates)
    weight, cumulative, offset = [v.reshape(heads, steps, group, Q) for v in (weight, cumulative, offset)]
    half = half.reshape(heads, steps, group, N)
    last_merge = merge.reshape(heads, steps, group * padded, N)[:, :, -padded:].reshape(heads, steps * padded, N)
    x_spec = pl.BlockSpec((rows, group * Q), lambda i, ids, *_: (0, ids[i]))
    span_spec = pl.BlockSpec((heads, None, group, Q), lambda i, ids, *_: (0, ids[i], 0, 0))
    level_spec = pl.BlockSpec((heads, group * padded, N), lambda i, ids, *_: (0, ids[i], 0))
    half_spec = pl.BlockSpec((heads, None, group, N), lambda i, ids, *_: (0, ids[i], 0, 0))
    low_slots = 2 * group
    vmem = pl.BlockSpec(memory_space=pltpu.VMEM)

    def within(start, count, base, trailing):
        return lambda i, *_: (jnp.clip(i - start, 0, count - 1) + base,) + (0,) * trailing

    def first_steps(id_lists):
        return [sum(ids.shape[0] for ids in id_lists[:at]) for at in range(len(id_lists))]

    totals, all_ids = [], []

    def states(sets):
        starts = first_steps([ids for ids, _ in sets])
        ids = join([ids for ids, _ in sets])
        count = ids.shape[0]
        key_specs = [
            pl.BlockSpec((block, N), within(start, own.shape[0], 0, 1)) for start, (own, _) in zip(starts, sets)
        ]
        low, total = pl.pallas_call(
            functools.partial(states_kernel, heads, width, group, padded, starts),
            grid_spec=pltpu.PrefetchScalarGridSpec(
                num_scalar_prefetch=2,
                grid=(count,),
                in_specs=[x_spec, span_spec, half_spec, level_spec] + [spec for spec in key_specs for _ in range(CORES)],
                out_specs=[
                    pl.BlockSpec((None, low_slots, rows, N), lambda i, *_: (i, 0, 0, 0)),
                    pl.BlockSpec((None, rows, N), lambda i, *_: (i, 0, 0)),
                ],
            ),
            out_shape=[
                jax.ShapeDtypeStruct((count, low_slots, rows, N), bf16),
                jax.ShapeDtypeStruct((count, rows, N), f32),
            ],
            compiler_params=params,
            cost_estimate=pl.CostEstimate(
                flops=2 * rows * count * group * Q * N,
                bytes_accessed=4 * count * group * Q * (rows + N),
                transcendentals=0,
            ),
            name="states",
        )(ids, core, x_heads, weight, half, merge, *[key for _, keys in sets for key in keys])
        totals.append(total)
        all_ids.append(ids)
        return [(low, start) for start in starts]

    def outputs(sets, out):
        starts = first_steps([ids for ids, *_ in sets])
        ids = join([ids for ids, *_ in sets])
        count = ids.shape[0]
        tokens_here = count * group * Q
        set_specs, operands = [], []
        for start, (own, keys, queries, (low, base)) in zip(starts, sets):
            set_specs += [pl.BlockSpec((block, N), within(start, own.shape[0], 0, 1))] * (2 * CORES)
            set_specs.append(pl.BlockSpec((None, low_slots, rows, N), within(start, own.shape[0], base, 3)))
            operands += [*keys, *queries, low]
        before = [] if out is None else [out]
        fixed = [
            pl.BlockSpec(memory_space=pltpu.SMEM),
            x_spec,
            vmem,
            span_spec,
            span_spec,
            level_spec,
            pl.BlockSpec(
                (1, heads * levels, group * Q),
                lambda i, ids, *_: (ids[i] // per_shard, 0, ids[i] % per_shard),
            ),
        ]

        def kernel(*refs):
            last = 2 + len(fixed) + len(set_specs)
            outputs_kernel(
                heads, width, group, bits, padded, starts, *refs[:last], *refs[last + len(before) :]
            )

        return pl.pallas_call(
            kernel,
            grid_spec=pltpu.PrefetchScalarGridSpec(
                num_scalar_prefetch=2,
                grid=(count,),
                in_specs=fixed + set_specs + [pl.BlockSpec(memory_space=pl.ANY)] * len(before),
                out_specs=x_spec,
                scratch_shapes=[
                    pltpu.VMEM((N, group * Q), bf16),
                    pltpu.VMEM((group, Q, HALF), f32),
                    pltpu.VMEM((rows, group * Q), f32),
                    pltpu.VMEM((heads, padded, group * Q), f32),
                    pltpu.VMEM((heads, 8, group * Q), f32),
                    pltpu.VMEM((group, heads, Q, HALF), bf16),
                ],
            ),
            out_shape=jax.ShapeDtypeStruct((rows, tokens), bf16),
            input_output_aliases={2 + len(fixed) + len(set_specs): 0} if before else {},
            compiler_params=params,
            cost_estimate=pl.CostEstimate(
                flops=2 * tokens_here * (Q * N + rows * Q + bits * rows * N),
                bytes_accessed=4 * tokens_here * (rows + N),
                transcendentals=heads * tokens_here * Q,
            ),
            name="outputs",
        )(ids, core, own_skip, x_heads, high, cumulative, offset, decay, level_rows, *operands, *before)

    here = join([group_ids(place, lax.axis_index("z").reshape(1)) for place in places()])
    one = (0, 0)
    sides = [place for place in places() if (place[0] > 0) != (place[1] > 0)]
    corners = [place for place in places() if place[0] and place[1]]
    far_ids = {place: group_ids(place) for place in places()}
    lows, cuts = {}, []
    if key_line:
        cut = block * ((len(key_line) + 1) // 3)
        by_x, by_y = slice(0, cut), slice(cut, None)
        key_far = straight(after(join(key_line), *crossed))
        keys_far = {one: with_core(key_far[one])}
        begun = [key_far[one]]
        low_here, lows[one] = states([(here, keys_here), (far_ids[one], keys_far[one])])
        query_line = along_z(after(c_proj, weight))
        if sides:
            tied = {place: after(key_far[place], totals[0]) for place in sides}
            parts = diagonal(tied, by_x, by_y, cuts)
            begun = [tied[place] for place in sides]
            keys_far.update({place: with_core(key_far[place]) for place in sides})
            lows.update(zip(sides, states([(far_ids[place], keys_far[place]) for place in sides])))
            if corners:
                joined = {place: join([after(part, *totals[:2]) for part in parts[place]]) for place in corners}
                begun = [joined[place] for place in corners]
                keys_far.update({place: with_core(joined[place]) for place in corners})
                lows.update(zip(corners, states([(far_ids[place], keys_far[place]) for place in corners])))
        query_far = straight(after(join(query_line), *begun))
    else:
        (low_here,) = states([(here, keys_here)])
    level_rows = lax.all_to_all(
        to_owners(after(level_weight, totals[0], *cuts).astype(bf16)), ("z", "y"), split_axis=0, concat_axis=0, tiled=True
    )
    queries_here = with_core(join([after(query_near[place], totals[0]) for place in places()]))

    high = pl.pallas_call(
        functools.partial(tree_kernel, width, group, padded),
        grid_spec=pltpu.PrefetchScalarGridSpec(
            num_scalar_prefetch=1,
            in_specs=[vmem] * (1 + len(totals)),
            out_specs=vmem,
            scratch_shapes=[pltpu.VMEM((steps, rows, N), f32)],
        ),
        out_shape=jax.ShapeDtypeStruct((steps, rows, N), bf16),
        compiler_params=params,
        name="tree",
    )(join(all_ids), last_merge, *totals)

    out = outputs([(here, keys_here, queries_here, low_here)], None)
    if key_line:
        tied = {place: after(query_far[place], out) for place in sides}
        parts = diagonal(tied, by_x, by_y)
        queries_far = {place: with_core(query_far[place] if place == one else tied[place]) for place in [one] + sides}
        for place in places():
            if sides and place == sides[-1]:
                for corner in corners:
                    queries_far[corner] = with_core(join([after(part, out) for part in parts[corner]]))
                out = after(out, *[queries_far[corner][0] for corner in corners])
            out = outputs([(far_ids[place], keys_far[place], queries_far[place], lows[place])], out)
    return out


def solution(mesh):
    x = mesh.shape["head"] // CORES
    y = math.gcd(mesh.shape["seq"], x)
    z = mesh.shape["seq"] // y
    split_mesh = jax.sharding.Mesh(mesh.devices.reshape(z, y, x, CORES), ("z", "y", "x", "core"))
    seq = ("z", "y")
    head = ("x", "core")
    in_specs = (
        P((*head, *seq), None),
        P((*seq, *head), None),
        P((*seq, *head), None),
        P(head, seq),
        P(head, seq),
        P(head, None, seq),
        P(head),
    )
    out_specs = P((*head, *seq), None)
    return jax.shard_map(
        on_device, mesh=split_mesh, in_specs=in_specs, out_specs=out_specs, check_vma=False
    )
```

profile of v0, /device:TPU:0, one launch (start us, length us, event | category | flops | bytes accessed | tf_op | source)
XLA Modules:
  0.0 198.6 jit_solution(3958275756563268738)
XLA Ops:
  0.0 2.9 %collective-permute-start = (bf16[1024,128]{1,0:T(8,128)(2,1)}, bf16[1024,128]{1,0:T(8,128)(2,1)S(1)}, u32[]{:S(2)}, u32[]{:S(2)}) collective-permute-start(bf16[1024,128]{1,0:T(8,128)(2,1)} %param.8), channel_id=1, source_target_pairs={{0,2},{2,0},{1,3},{3,1},{4,6},{6,4},{5,7},{7,5},{8,10},{10,8},{9,1... | collective-permute-start | bytes 786440 | tf_op jit(solution)/shard_map/ppermute | solution.py:231
  2.9 2.6 %collective-permute-start.5 = (bf16[1024,128]{1,0:T(8,128)(2,1)}, bf16[1024,128]{1,0:T(8,128)(2,1)S(1)}, u32[]{:S(2)}, u32[]{:S(2)}) collective-permute-start(bf16[1024,128]{1,0:T(8,128)(2,1)} %param.8), channel_id=1, source_target_pairs={{0,16},{8,24},{16,0},{24,8},{1,17},{9,25},{17,1},{25,9},{2,18},{10... | collective-permute-start | bytes 786440 | tf_op jit(solution)/shard_map/ppermute | solution.py:231
  5.5 1.5 collective-permute-start.1
  7.0 1.6 collective-permute-start.4
  9.5 1.8 collective-permute-start.2
  11.2 1.0 constant_dynamic-update-slice_fusion.3
  12.2 1.0 copy.14
  13.2 1.0 copy.15
  14.3 3.3 %collective-permute-done.5 = bf16[1024,128]{1,0:T(8,128)(2,1)S(1)} collective-permute-done((bf16[1024,128]{1,0:T(8,128)(2,1)}, bf16[1024,128]{1,0:T(8,128)(2,1)S(1)}, u32[]{:S(2)}, u32[]{:S(2)}) %collective-permute-start.5) | collective-permute-done | bytes 262176 | tf_op jit(solution)/shard_map/ppermute | solution.py:231
  18.9 5.5 %collective-permute-done.2 = bf16[1024,128]{1,0:T(8,128)(2,1)S(1)} collective-permute-done((bf16[1024,128]{1,0:T(8,128)(2,1)S(1)}, bf16[1024,128]{1,0:T(8,128)(2,1)S(1)}, u32[]{:S(2)}, u32[]{:S(2)}) %collective-permute-start.2) | collective-permute-done | bytes 262176 | tf_op jit(solution)/shard_map/ppermute | solution.py:231
  25.6 1.0 collective-permute-done.7
  26.6 1.5 collective-permute-start.12
  29.5 4.7 %all-to-all-start = ((f32[8,4,16,256]{3,2,1,0:T(8,128)}), f32[8,4,16,256]{3,2,1,0:T(8,128)}, u32[]{:S(2)}, u32[]{:S(2)}) async-start(f32[8,4,16,256]{3,2,1,0:T(8,128)} %bitcast.41), calls=%async_computation | async-start | bytes 1048576 | tf_op jit(solution)/shard_map/all_to_all | solution.py:321
  34.2 12.4 %collective-permute-done.10.refs_0_.refs_9_ = bf16[3072,128]{1,0:T(8,128)(2,1)S(1)} collective-permute-done((bf16[3072,128]{1,0:T(8,128)(2,1)S(1)}, bf16[3072,128]{1,0:T(8,128)(2,1)S(1)}, u32[]{:S(2)}, u32[]{:S(2)}) %collective-permute-start.10) | collective-permute-done | bytes 786464 | tf_op jit(solution)/shard_map/ppermute | solution.py:231
  46.6 3.7 %collective-permute-done.12.refs_2_.refs_9_ = bf16[3072,128]{1,0:T(8,128)(2,1)S(1)} collective-permute-done((bf16[3072,128]{1,0:T(8,128)(2,1)S(1)}, bf16[3072,128]{1,0:T(8,128)(2,1)S(1)}, u32[]{:S(2)}, u32[]{:S(2)}) %collective-permute-start.12) | collective-permute-done | bytes 786464 | tf_op jit(solution)/shard_map/ppermute | solution.py:231
  51.7 5.3 %gates.1 = (f32[2,128,256]{2,1,0:T(8,128)}, f32[2,128,256]{2,1,0:T(8,128)}, f32[2,128,256]{2,1,0:T(8,128)}, f32[2,128,128]{2,1,0:T(8,128)}, f32[2,1024,128]{2,1,0:T(8,128)}, /*index=5*/f32[2,1024,128]{2,1,0:T(8,128)}) custom-call(f32[8,4,16,256]{3,2,1,0:T(8,128)} %all-to-all-done.gates_ref), custom_call_target="tpu_custom_call" | custom-call | tf_op jit(solution)/shard_map/gates/pallas_call | solution.py:330
  57.0 9.0 %states.3 = (bf16[7,16,128,128]{3,2,1,0:T(8,128)(2,1)}, f32[7,128,128]{2,1,0:T(8,128)}) custom-call(s32[7]{0:T(128)} %concatenate.33.groups_ref, s32[1]{0:T(128)} %bitcast.core_ref.refs_1_, bf16[128,32768]{1,0:T(8,128)(2,1)} %refs_3_.9, f32[2,16,8,256]{3,2,1,0:T(8,128)} %bitcast.38, f32[2,16,8,128]{3,2,1,0:T(8,128)} %bitcast.42, ...), custom_call_target="tpu_custom_call" | custom-call | flops 469762048 | bytes 14680064 | tf_op jit(solution)/shard_map/states/pallas_call | solution.py:364
  66.8 2.8 %convert_element_type.3 = bf16[16,8,4096]{2,1,0:T(8,128)(2,1)} convert(f32[16,8,4096]{2,1,0:T(8,128)} %param.12) | non-fusion elementwise | flops 524288 | bytes 3145728 | tf_op jit(solution)/shard_map/convert_element_type | solution.py:477
  69.5 5.7 %all-to-all-start.1 = ((bf16[8,16,4096]{2,1,0:T(8,128)(2,1)}), bf16[8,16,4096]{2,1,0:T(8,128)(2,1)S(1)}, u32[]{:S(2)}, u32[]{:S(2)}) async-start(bf16[8,16,4096]{2,1,0:T(8,128)(2,1)} %bitcast.37), calls=%async_computation.1 | async-start | bytes 2097152 | tf_op jit(solution)/shard_map/all_to_all | solution.py:476
  75.8 2.9 %collective-permute-start.18 = (bf16[1024,128]{1,0:T(8,128)(2,1)}, bf16[1024,128]{1,0:T(8,128)(2,1)}, u32[]{:S(2)}, u32[]{:S(2)}) collective-permute-start(bf16[1024,128]{1,0:T(8,128)(2,1)} %param.9), channel_id=1, source_target_pairs={{0,16},{8,24},{16,0},{24,8},{1,17},{9,25},{17,1},{25,9},{2,18},{10... | collective-permute-start | bytes 786440 | tf_op jit(solution)/shard_map/ppermute | solution.py:231
  78.8 1.5 collective-permute-start.15
  80.3 1.7 constant_dynamic-update-slice_fusion.9
  81.9 1.7 constant_dynamic-update-slice_fusion.8
  83.6 1.4 collective-permute-start.14
  85.8 1.7 constant_dynamic-update-slice_fusion.6.refs_11_
  87.5 25.1 %collective-permute-done.18 = bf16[1024,128]{1,0:T(8,128)(2,1)} collective-permute-done((bf16[1024,128]{1,0:T(8,128)(2,1)}, bf16[1024,128]{1,0:T(8,128)(2,1)}, u32[]{:S(2)}, u32[]{:S(2)}) %collective-permute-start.18) | collective-permute-done | bytes 262176 | tf_op jit(solution)/shard_map/ppermute | solution.py:231
  112.6 2.0 %collective-permute-start.19 = (bf16[1024,128]{1,0:T(8,128)(2,1)}, bf16[1024,128]{1,0:T(8,128)(2,1)}, u32[]{:S(2)}, u32[]{:S(2)}) collective-permute-start(bf16[1024,128]{1,0:T(8,128)(2,1)} %collective-permute-done.18), channel_id=1, source_target_pairs={{0,8},{8,0},{16,24},{24,16},{1,9},{9,1},{17,25},{25,17},{2,10},{10... | collective-permute-start | bytes 786440 | tf_op jit(solution)/shard_map/ppermute | solution.py:231
  114.6 7.9 %states.4 = (bf16[6,16,128,128]{3,2,1,0:T(8,128)(2,1)}, f32[6,128,128]{2,1,0:T(8,128)}) custom-call(s32[6]{0:T(128)} %pad_add_fusion.groups_ref, s32[1]{0:T(128)} %bitcast.core_ref.refs_1_, bf16[128,32768]{1,0:T(8,128)(2,1)} %refs_3_.9, f32[2,16,8,256]{3,2,1,0:T(8,128)} %bitcast.39, f32[2,16,8,128]{3,2,1,0:T(8,128)} %bitcast.43, ...), custom_call_target="tpu_custom_call" | custom-call | flops 402653184 | bytes 12582912 | tf_op jit(solution)/shard_map/states/pallas_call | solution.py:364
  122.5 1.0 constant_dynamic-update-slice_fusion.5
  124.1 1.5 collective-permute-done.19
  125.6 1.2 pad_maximum_fusion.1.refs_11_
  126.8 1.6 collective-permute-start.20
  130.2 1.6 collective-permute-start.26
  131.8 1.6 slice_bitcast_fusion.merge_ref
  133.4 0.9 copy-done.7
  134.3 5.2 %states.5 = (bf16[3,16,128,128]{3,2,1,0:T(8,128)(2,1)}, f32[3,128,128]{2,1,0:T(8,128)}) custom-call(s32[3]{0:T(128)} %copy-done.14, s32[1]{0:T(128)} %bitcast.core_ref.refs_1_, bf16[128,32768]{1,0:T(8,128)(2,1)} %refs_3_.9, f32[2,16,8,256]{3,2,1,0:T(8,128)} %bitcast.40, f32[2,16,8,128]{3,2,1,0:T(8,128)} %bitcast.44, ...), custom_call_target="tpu_custom_call" | custom-call | flops 201326592 | bytes 6291456 | tf_op jit(solution)/shard_map/states/pallas_call | solution.py:364
  139.5 2.9 %tree.1.refs_4_ = bf16[16,128,128]{2,1,0:T(8,128)(2,1)} custom-call(s32[16]{0:T(128)} %concatenate.32.groups_ref, f32[2,128,128]{2,1,0:T(8,128)} %slice_bitcast_fusion.merge_ref, f32[7,128,128]{2,1,0:T(8,128)} %get-tuple-element.38.refs_0_, f32[6,128,128]{2,1,0:T(8,128)} %get-tuple-element.39.refs_1_, f32[3,128,128]{2,1,0:T(8,128)} %get-tuple-element.44.refs_2_), custom_call_target="tpu_custom_call" | custom-call | tf_op jit(solution)/shard_map/tree/pallas_call | solution.py:481
  142.4 1.0 copy-done
  143.4 11.3 %outputs.5.refs_14_ = bf16[128,32768]{1,0:T(8,128)(2,1)} custom-call(s32[4]{0:T(128)} %pad_add_fusion.1.refs_0_, s32[1]{0:T(128)} %bitcast.core_ref.refs_1_, f32[2]{0:T(128)} %dynamic_slice.3.refs_2_, bf16[128,32768]{1,0:T(8,128)(2,1)} %refs_3_.9, bf16[16,128,128]{2,1,0:T(8,128)(2,1)} %tree.1.refs_4_, f32[2,16,8,256]{3,2,1,0:T(8,128)} %bitcast.27, ...), custom_call_target="tpu_custom_call" | custom-call | flops 2952790016 | bytes 8388608 | tf_op jit(solution)/shard_map/outputs/pallas_call | solution.py:421
  155.3 1.1 slice.19
  156.9 1.0 slice.18
  158.5 9.3 %outputs.6.refs_14_ = bf16[128,32768]{1,0:T(8,128)(2,1)} custom-call(s32[3]{0:T(128)} %copy-done.15, s32[1]{0:T(128)} %bitcast.core_ref.refs_1_, f32[2]{0:T(128)} %dynamic_slice.3.refs_2_, bf16[128,32768]{1,0:T(8,128)(2,1)} %refs_3_.9, bf16[16,128,128]{2,1,0:T(8,128)(2,1)} %tree.1.refs_4_, ...), custom_call_target="tpu_custom_call", output_to_operand_aliasing={{}: (14, {})} | custom-call | flops 2214592512 | bytes 6291456 | tf_op jit(solution)/shard_map/outputs/pallas_call | solution.py:421
  167.8 0.9 copy-done.10
  168.7 9.2 %outputs.7.refs_14_ = bf16[128,32768]{1,0:T(8,128)(2,1)} custom-call(s32[3]{0:T(128)} %copy-done.17, s32[1]{0:T(128)} %bitcast.core_ref.refs_1_, f32[2]{0:T(128)} %dynamic_slice.3.refs_2_, bf16[128,32768]{1,0:T(8,128)(2,1)} %refs_3_.9, bf16[16,128,128]{2,1,0:T(8,128)(2,1)} %tree.1.refs_4_, ...), custom_call_target="tpu_custom_call", output_to_operand_aliasing={{}: (14, {})} | custom-call | flops 2214592512 | bytes 6291456 | tf_op jit(solution)/shard_map/outputs/pallas_call | solution.py:421
  178.2 1.0 copy-done.9
  179.2 9.3 %outputs.8.refs_14_ = bf16[128,32768]{1,0:T(8,128)(2,1)} custom-call(s32[3]{0:T(128)} %copy-done.16, s32[1]{0:T(128)} %bitcast.core_ref.refs_1_, f32[2]{0:T(128)} %dynamic_slice.3.refs_2_, bf16[128,32768]{1,0:T(8,128)(2,1)} %refs_3_.9, bf16[16,128,128]{2,1,0:T(8,128)(2,1)} %tree.1.refs_4_, ...), custom_call_target="tpu_custom_call", output_to_operand_aliasing={{}: (14, {})} | custom-call | flops 2214592512 | bytes 6291456 | tf_op jit(solution)/shard_map/outputs/pallas_call | solution.py:421
  188.5 0.9 copy-done.11
  189.4 9.2 %outputs.9 = bf16[128,32768]{1,0:T(8,128)(2,1)} custom-call(s32[3]{0:T(128)} %copy-done.14, s32[1]{0:T(128)} %bitcast.core_ref.refs_1_, f32[2]{0:T(128)} %dynamic_slice.3.refs_2_, bf16[128,32768]{1,0:T(8,128)(2,1)} %refs_3_.9, bf16[16,128,128]{2,1,0:T(8,128)(2,1)} %tree.1.refs_4_, f32[2,16,8,256]{3,2,1,0:T(8,128)} %bitcast.31, ...), custom_call_target="tpu_custom_call", output_to_operand_aliasing={{}: (14, {})} | custom-call | flops 2214592512 | bytes 6291456 | tf_op jit(solution)/shard_map/outputs/pallas_call | solution.py:421
  (96 shorter events, 12.8 us)
Async XLA Ops:
  0.0 9.5 %collective-permute-start = (bf16[1024,128]{1,0:T(8,128)(2,1)}, bf16[1024,128]{1,0:T(8,128)(2,1)S(1)}, u32[]{:S(2)}, u32[]{:S(2)}) collective-permute-start(bf16[1024,128]{1,0:T(8,128)(2,1)} %param.8), channel_id=1, source_target_pairs={{0,2},{2,0},{1,3},{3,1},{4,6},{6,4},{5,7},{7,5},{8,10},{10,8},{9,1... | collective-permute-start | bytes 786440 | tf_op jit(solution)/shard_map/ppermute | solution.py:231
  2.9 14.6 %collective-permute-start.5 = (bf16[1024,128]{1,0:T(8,128)(2,1)}, bf16[1024,128]{1,0:T(8,128)(2,1)S(1)}, u32[]{:S(2)}, u32[]{:S(2)}) collective-permute-start(bf16[1024,128]{1,0:T(8,128)(2,1)} %param.8), channel_id=1, source_target_pairs={{0,16},{8,24},{16,0},{24,8},{1,17},{9,25},{17,1},{25,9},{2,18},{10... | collective-permute-start | bytes 786440 | tf_op jit(solution)/shard_map/ppermute | solution.py:231
  5.5 12.8 %collective-permute-start.1 = (bf16[1024,128]{1,0:T(8,128)(2,1)}, bf16[1024,128]{1,0:T(8,128)(2,1)S(1)}, u32[]{:S(2)}, u32[]{:S(2)}) collective-permute-start(bf16[1024,128]{1,0:T(8,128)(2,1)} %param.8), channel_id=1, source_target_pairs={{0,4},{4,0},{1,5},{5,1},{2,6},{6,2},{3,7},{7,3},{8,12},{12,8},{9,1... | collective-permute-start | bytes 786440 | tf_op jit(solution)/shard_map/ppermute | solution.py:231
  7.0 17.5 %collective-permute-start.4 = (bf16[1024,128]{1,0:T(8,128)(2,1)}, bf16[1024,128]{1,0:T(8,128)(2,1)S(1)}, u32[]{:S(2)}, u32[]{:S(2)}) collective-permute-start(bf16[1024,128]{1,0:T(8,128)(2,1)} %param.8), channel_id=1, source_target_pairs={{0,8},{8,0},{16,24},{24,16},{1,9},{9,1},{17,25},{25,17},{2,10},{10... | collective-permute-start | bytes 786440 | tf_op jit(solution)/shard_map/ppermute | solution.py:231
  8.6 16.2 %collective-permute-start.8 = (bf16[1024,128]{1,0:T(8,128)(2,1)}, bf16[1024,128]{1,0:T(8,128)(2,1)S(1)}, u32[]{:S(2)}, u32[]{:S(2)}) collective-permute-start(bf16[1024,128]{1,0:T(8,128)(2,1)} %param.9), channel_id=1, source_target_pairs={{0,4},{4,0},{1,5},{5,1},{2,6},{6,2},{3,7},{7,3},{8,12},{12,8},{9,1... | collective-permute-start | bytes 786440 | tf_op jit(solution)/shard_map/ppermute | solution.py:231
  9.5 15.0 %collective-permute-start.2 = (bf16[1024,128]{1,0:T(8,128)(2,1)S(1)}, bf16[1024,128]{1,0:T(8,128)(2,1)S(1)}, u32[]{:S(2)}, u32[]{:S(2)}) collective-permute-start(bf16[1024,128]{1,0:T(8,128)(2,1)S(1)} %collective-permute-done), channel_id=1, source_target_pairs={{0,4},{4,0},{1,5},{5,1},{2,6},{6,2},{3,7},{7,3},{8,12},{12,8},{9,1... | collective-permute-start | bytes 786440 | tf_op jit(solution)/shard_map/ppermute | solution.py:231
  17.6 7.2 %collective-permute-start.6 = (bf16[1024,128]{1,0:T(8,128)(2,1)S(1)}, bf16[1024,128]{1,0:T(8,128)(2,1)S(1)}, u32[]{:S(2)}, u32[]{:S(2)}) collective-permute-start(bf16[1024,128]{1,0:T(8,128)(2,1)S(1)} %collective-permute-done.5), channel_id=1, source_target_pairs={{0,8},{8,0},{16,24},{24,16},{1,9},{9,1},{17,25},{25,17},{2,10},{10... | collective-permute-start | bytes 786440 | tf_op jit(solution)/shard_map/ppermute | solution.py:231
  18.3 8.3 %collective-permute-start.7 = (bf16[1024,128]{1,0:T(8,128)(2,1)}, bf16[1024,128]{1,0:T(8,128)(2,1)}, u32[]{:S(2)}, u32[]{:S(2)}) collective-permute-start(bf16[1024,128]{1,0:T(8,128)(2,1)} %param.9), channel_id=1, source_target_pairs={{0,2},{2,0},{1,3},{3,1},{4,6},{6,4},{5,7},{7,5},{8,10},{10,8},{9,1... | collective-permute-start | bytes 786440 | tf_op jit(solution)/shard_map/ppermute | solution.py:231
  24.5 5.0 %copy-start.3 = (bf16[4096,128]{1,0:T(8,128)(2,1)}, bf16[4096,128]{1,0:T(8,128)(2,1)S(1)}, u32[]{:S(2)}) copy-start(bf16[4096,128]{1,0:T(8,128)(2,1)S(1)} %constant_dynamic-update-slice_fusion.refs_0_.refs_9_) | copy-start | bytes 3145732
  24.5 32.5 %collective-permute-start.3 = (bf16[4096,128]{1,0:T(8,128)(2,1)S(1)}, bf16[4096,128]{1,0:T(8,128)(2,1)}, u32[]{:S(2)}, u32[]{:S(2)}) collective-permute-start(bf16[4096,128]{1,0:T(8,128)(2,1)S(1)} %constant_dynamic-update-slice_fusion.refs_0_.refs_9_), channel_id=1, source_target_pairs={{0,1},{1,0},{2,3},{3,2},{4,5},{5,4},{6,7},{7,6},{8,9},{9,8},{10,11... | collective-permute-start | bytes 3145736 | tf_op jit(solution)/shard_map/ppermute | solution.py:231
  24.8 32.2 %copy-start.1 = (bf16[3072,128]{1,0:T(8,128)(2,1)}, bf16[3072,128]{1,0:T(8,128)(2,1)S(1)}, u32[]{:S(2)}) copy-start(bf16[3072,128]{1,0:T(8,128)(2,1)S(1)} %pad_maximum_fusion.refs_2_.refs_9_) | copy-start | bytes 2359300
  26.6 23.7 %collective-permute-start.12 = (bf16[3072,128]{1,0:T(8,128)(2,1)S(1)}, bf16[3072,128]{1,0:T(8,128)(2,1)S(1)}, u32[]{:S(2)}, u32[]{:S(2)}) collective-permute-start(bf16[3072,128]{1,0:T(8,128)(2,1)S(1)} %pad_maximum_fusion.refs_2_.refs_9_), channel_id=1, source_target_pairs={{0,4},{4,0},{1,5},{5,1},{2,6},{6,2},{3,7},{7,3},{8,12},{12,8},{9,1... | collective-permute-start | bytes 2359304 | tf_op jit(solution)/shard_map/ppermute | solution.py:231
  28.1 18.5 %collective-permute-start.10 = (bf16[3072,128]{1,0:T(8,128)(2,1)S(1)}, bf16[3072,128]{1,0:T(8,128)(2,1)S(1)}, u32[]{:S(2)}, u32[]{:S(2)}) collective-permute-start(bf16[3072,128]{1,0:T(8,128)(2,1)S(1)} %pad_maximum_fusion.refs_2_.refs_9_), channel_id=1, source_target_pairs={{0,2},{2,0},{1,3},{3,1},{4,6},{6,4},{5,7},{7,5},{8,10},{10,8},{9,1... | collective-permute-start | bytes 2359304 | tf_op jit(solution)/shard_map/ppermute | solution.py:231
  29.5 22.2 %all-to-all-start = ((f32[8,4,16,256]{3,2,1,0:T(8,128)}), f32[8,4,16,256]{3,2,1,0:T(8,128)}, u32[]{:S(2)}, u32[]{:S(2)}) async-start(f32[8,4,16,256]{3,2,1,0:T(8,128)} %bitcast.41), calls=%async_computation | async-start | bytes 1048576 | tf_op jit(solution)/shard_map/all_to_all | solution.py:321
  34.2 22.8 %collective-permute-start.9 = (bf16[3072,128]{1,0:T(8,128)(2,1)S(1)}, bf16[3072,128]{1,0:T(8,128)(2,1)}, u32[]{:S(2)}, u32[]{:S(2)}) collective-permute-start(bf16[3072,128]{1,0:T(8,128)(2,1)S(1)} %pad_maximum_fusion.refs_2_.refs_9_), channel_id=1, source_target_pairs={{0,1},{1,0},{2,3},{3,2},{4,5},{5,4},{6,7},{7,6},{8,9},{9,8},{10,11... | collective-permute-start | bytes 2359304 | tf_op jit(solution)/shard_map/ppermute | solution.py:231
  34.2 94.2 %copy-start.15 = (s32[3]{0:T(128)}, s32[3]{0:T(128)S(1)}, u32[]{:S(2)}) copy-start(s32[3]{0:T(128)S(1)} %broadcast_add_fusion.1.refs_0_) | copy-start | bytes 40
  46.6 19.4 %copy-start.4 = (bf16[3072,128]{1,0:T(8,128)(2,1)}, bf16[3072,128]{1,0:T(8,128)(2,1)S(1)}, u32[]{:S(2)}) copy-start(bf16[3072,128]{1,0:T(8,128)(2,1)S(1)} %collective-permute-done.10.refs_0_.refs_9_) | copy-start | bytes 2359300
  46.6 65.9 %collective-permute-start.11 = (bf16[3072,128]{1,0:T(8,128)(2,1)S(1)}, bf16[3072,128]{1,0:T(8,128)(2,1)}, u32[]{:S(2)}, u32[]{:S(2)}) collective-permute-start(bf16[3072,128]{1,0:T(8,128)(2,1)S(1)} %collective-permute-done.10.refs_0_.refs_9_), channel_id=1, source_target_pairs={{0,1},{1,0},{2,3},{3,2},{4,5},{5,4},{6,7},{7,6},{8,9},{9,8},{10,11... | collective-permute-start | bytes 2359304 | tf_op jit(solution)/shard_map/ppermute | solution.py:231
  50.3 15.7 %copy-start.2 = (bf16[3072,128]{1,0:T(8,128)(2,1)}, bf16[3072,128]{1,0:T(8,128)(2,1)S(1)}, u32[]{:S(2)}) copy-start(bf16[3072,128]{1,0:T(8,128)(2,1)S(1)} %collective-permute-done.12.refs_2_.refs_9_) | copy-start | bytes 2359300
  50.3 64.3 %collective-permute-start.13 = (bf16[3072,128]{1,0:T(8,128)(2,1)S(1)}, bf16[3072,128]{1,0:T(8,128)(2,1)}, u32[]{:S(2)}, u32[]{:S(2)}) collective-permute-start(bf16[3072,128]{1,0:T(8,128)(2,1)S(1)} %collective-permute-done.12.refs_2_.refs_9_), channel_id=1, source_target_pairs={{0,1},{1,0},{2,3},{3,2},{4,5},{5,4},{6,7},{7,6},{8,9},{9,8},{10,11... | collective-permute-start | bytes 2359304 | tf_op jit(solution)/shard_map/ppermute | solution.py:231
  50.3 78.0 %copy-start.17 = (s32[3]{0:T(128)}, s32[3]{0:T(128)S(1)}, u32[]{:S(2)}) copy-start(s32[3]{0:T(128)S(1)} %broadcast_add_fusion.2.refs_0_) | copy-start | bytes 40
  51.1 77.2 %copy-start.16 = (s32[3]{0:T(128)}, s32[3]{0:T(128)S(1)}, u32[]{:S(2)}) copy-start(s32[3]{0:T(128)S(1)} %broadcast_add_fusion.refs_0_) | copy-start | bytes 40
  51.1 32.5 %collective-permute-start.21 = (bf16[1024,128]{1,0:T(8,128)(2,1)}, bf16[1024,128]{1,0:T(8,128)(2,1)}, u32[]{:S(2)}, u32[]{:S(2)}) collective-permute-start(bf16[1024,128]{1,0:T(8,128)(2,1)} %copy-done.12), channel_id=1, source_target_pairs={{0,2},{2,0},{1,3},{3,1},{4,6},{6,4},{5,7},{7,5},{8,10},{10,8},{9,1... | collective-permute-start | bytes 786440 | tf_op jit(solution)/shard_map/ppermute | solution.py:231
  69.5 15.5 %copy-start.13 = (bf16[1024,128]{1,0:T(8,128)(2,1)S(1)}, bf16[1024,128]{1,0:T(8,128)(2,1)}, u32[]{:S(2)}) copy-start(bf16[1024,128]{1,0:T(8,128)(2,1)} %copy-done.12) | copy-start | bytes 786436
  69.5 72.9 %all-to-all-start.1 = ((bf16[8,16,4096]{2,1,0:T(8,128)(2,1)}), bf16[8,16,4096]{2,1,0:T(8,128)(2,1)S(1)}, u32[]{:S(2)}, u32[]{:S(2)}) async-start(bf16[8,16,4096]{2,1,0:T(8,128)(2,1)} %bitcast.37), calls=%async_computation.1 | async-start | bytes 2097152 | tf_op jit(solution)/shard_map/all_to_all | solution.py:476
  75.8 36.7 %collective-permute-start.18 = (bf16[1024,128]{1,0:T(8,128)(2,1)}, bf16[1024,128]{1,0:T(8,128)(2,1)}, u32[]{:S(2)}, u32[]{:S(2)}) collective-permute-start(bf16[1024,128]{1,0:T(8,128)(2,1)} %param.9), channel_id=1, source_target_pairs={{0,16},{8,24},{16,0},{24,8},{1,17},{9,25},{17,1},{25,9},{2,18},{10... | collective-permute-start | bytes 786440 | tf_op jit(solution)/shard_map/ppermute | solution.py:231
  78.8 44.7 %collective-permute-start.15 = (bf16[2048,128]{1,0:T(8,128)(2,1)S(1)}, bf16[2048,128]{1,0:T(8,128)(2,1)S(1)}, u32[]{:S(2)}, u32[]{:S(2)}) collective-permute-start(bf16[2048,128]{1,0:T(8,128)(2,1)S(1)} %slice.17), channel_id=1, source_target_pairs={{0,2},{2,0},{1,3},{3,1},{4,6},{6,4},{5,7},{7,5},{8,10},{10,8},{9,1... | collective-permute-start | bytes 1572872 | tf_op jit(solution)/shard_map/ppermute | solution.py:231
  83.6 38.8 %collective-permute-start.14 = (bf16[1024,128]{1,0:T(8,128)(2,1)}, bf16[1024,128]{1,0:T(8,128)(2,1)}, u32[]{:S(2)}, u32[]{:S(2)}) collective-permute-start(bf16[1024,128]{1,0:T(8,128)(2,1)} %slice.16), channel_id=1, source_target_pairs={{0,4},{4,0},{1,5},{5,1},{2,6},{6,2},{3,7},{7,3},{8,12},{12,8},{9,1... | collective-permute-start | bytes 786440 | tf_op jit(solution)/shard_map/ppermute | solution.py:231
  112.6 11.6 %collective-permute-start.17 = (bf16[1024,128]{1,0:T(8,128)(2,1)}, bf16[1024,128]{1,0:T(8,128)(2,1)}, u32[]{:S(2)}, u32[]{:S(2)}) collective-permute-start(bf16[1024,128]{1,0:T(8,128)(2,1)} %param.9), channel_id=1, source_target_pairs={{0,8},{8,0},{16,24},{24,16},{1,9},{9,1},{17,25},{25,17},{2,10},{10... | collective-permute-start | bytes 786440 | tf_op jit(solution)/shard_map/ppermute | solution.py:231
  112.6 13.0 %collective-permute-start.19 = (bf16[1024,128]{1,0:T(8,128)(2,1)}, bf16[1024,128]{1,0:T(8,128)(2,1)}, u32[]{:S(2)}, u32[]{:S(2)}) collective-permute-start(bf16[1024,128]{1,0:T(8,128)(2,1)} %collective-permute-done.18), channel_id=1, source_target_pairs={{0,8},{8,0},{16,24},{24,16},{1,9},{9,1},{17,25},{25,17},{2,10},{10... | collective-permute-start | bytes 786440 | tf_op jit(solution)/shard_map/ppermute | solution.py:231
  114.6 27.8 %collective-permute-start.22 = (bf16[4096,128]{1,0:T(8,128)(2,1)}, bf16[4096,128]{1,0:T(8,128)(2,1)}, u32[]{:S(2)}, u32[]{:S(2)}) collective-permute-start(bf16[4096,128]{1,0:T(8,128)(2,1)} %constant_dynamic-update-slice_fusion.6.refs_11_), channel_id=1, source_target_pairs={{0,1},{1,0},{2,3},{3,2},{4,5},{5,4},{6,7},{7,6},{8,9},{9,8},{10,11... | collective-permute-start | bytes 3145736 | tf_op jit(solution)/shard_map/ppermute | solution.py:231
  122.5 6.6 %copy-start.18 = (f32[16]{0:T(128)S(1)}, f32[16]{0:T(128)}, u32[]{:S(2)}) copy-start(f32[16]{0:T(128)} %param.13) | copy-start | bytes 196
  123.6 9.9 %copy-start.5 = (bf16[3072,128]{1,0:T(8,128)(2,1)}, bf16[3072,128]{1,0:T(8,128)(2,1)S(1)}, u32[]{:S(2)}) copy-start(bf16[3072,128]{1,0:T(8,128)(2,1)S(1)} %constant_dynamic-update-slice_fusion.4.refs_0_.refs_9_) | copy-start | bytes 2359300
  123.6 9.8 %collective-permute-start.16 = (bf16[3072,128]{1,0:T(8,128)(2,1)S(1)}, bf16[3072,128]{1,0:T(8,128)(2,1)S(1)}, u32[]{:S(2)}, u32[]{:S(2)}) collective-permute-start(bf16[3072,128]{1,0:T(8,128)(2,1)S(1)} %constant_dynamic-update-slice_fusion.4.refs_0_.refs_9_), channel_id=1, source_target_pairs={{0,1},{1,0},{2,3},{3,2},{4,5},{5,4},{6,7},{7,6},{8,9},{9,8},{10,11... | collective-permute-start | bytes 2359304 | tf_op jit(solution)/shard_map/ppermute | solution.py:231
  126.8 12.7 %copy-start.6 = (bf16[3072,128]{1,0:T(8,128)(2,1)}, bf16[3072,128]{1,0:T(8,128)(2,1)S(1)}, u32[]{:S(2)}) copy-start(bf16[3072,128]{1,0:T(8,128)(2,1)S(1)} %pad_maximum_fusion.1.refs_11_) | copy-start | bytes 2359300
  126.8 27.9 %collective-permute-start.20 = (bf16[3072,128]{1,0:T(8,128)(2,1)S(1)}, bf16[3072,128]{1,0:T(8,128)(2,1)}, u32[]{:S(2)}, u32[]{:S(2)}) collective-permute-start(bf16[3072,128]{1,0:T(8,128)(2,1)S(1)} %pad_maximum_fusion.1.refs_11_), channel_id=1, source_target_pairs={{0,2},{2,0},{1,3},{3,1},{4,6},{6,4},{5,7},{7,5},{8,10},{10,8},{9,1... | collective-permute-start | bytes 2359304 | tf_op jit(solution)/shard_map/ppermute | solution.py:231
  128.4 5.0 %copy-start.14 = (s32[3]{0:T(128)}, s32[3]{0:T(128)S(1)}, u32[]{:S(2)}) copy-start(s32[3]{0:T(128)S(1)} %broadcast_add_fusion.3.groups_ref.refs_0_) | copy-start | bytes 40
  130.2 25.0 %collective-permute-start.26 = (bf16[3072,128]{1,0:T(8,128)(2,1)S(1)}, bf16[3072,128]{1,0:T(8,128)(2,1)}, u32[]{:S(2)}, u32[]{:S(2)}) collective-permute-start(bf16[3072,128]{1,0:T(8,128)(2,1)S(1)} %pad_maximum_fusion.1.refs_11_), channel_id=1, source_target_pairs={{0,4},{4,0},{1,5},{5,1},{2,6},{6,2},{3,7},{7,3},{8,12},{12,8},{9,1... | collective-permute-start | bytes 2359304 | tf_op jit(solution)/shard_map/ppermute | solution.py:231
  133.4 25.1 %collective-permute-start.25 = (bf16[3072,128]{1,0:T(8,128)(2,1)S(1)}, bf16[3072,128]{1,0:T(8,128)(2,1)}, u32[]{:S(2)}, u32[]{:S(2)}) collective-permute-start(bf16[3072,128]{1,0:T(8,128)(2,1)S(1)} %pad_maximum_fusion.1.refs_11_), channel_id=1, source_target_pairs={{0,1},{1,0},{2,3},{3,2},{4,5},{5,4},{6,7},{7,6},{8,9},{9,8},{10,11... | collective-permute-start | bytes 2359304 | tf_op jit(solution)/shard_map/ppermute | solution.py:231
  142.4 1.0 copy-start
  154.7 13.1 %collective-permute-start.24 = (bf16[3072,128]{1,0:T(8,128)(2,1)}, bf16[3072,128]{1,0:T(8,128)(2,1)S(1)}, u32[]{:S(2)}, u32[]{:S(2)}) collective-permute-start(bf16[3072,128]{1,0:T(8,128)(2,1)} %collective-permute-done.20.refs_11_), channel_id=1, source_target_pairs={{0,1},{1,0},{2,3},{3,2},{4,5},{5,4},{6,7},{7,6},{8,9},{9,8},{10,11... | collective-permute-start | bytes 2359304 | tf_op jit(solution)/shard_map/ppermute | solution.py:231
  156.4 21.5 %collective-permute-start.27 = (bf16[2048,128]{1,0:T(8,128)(2,1)S(1)}, bf16[2048,128]{1,0:T(8,128)(2,1)S(1)}, u32[]{:S(2)}, u32[]{:S(2)}) collective-permute-start(bf16[2048,128]{1,0:T(8,128)(2,1)S(1)} %slice.19), channel_id=1, source_target_pairs={{0,2},{2,0},{1,3},{3,1},{4,6},{6,4},{5,7},{7,5},{8,10},{10,8},{9,1... | collective-permute-start | bytes 1572872 | tf_op jit(solution)/shard_map/ppermute | solution.py:231
  157.9 20.3 %collective-permute-start.29 = (bf16[3072,128]{1,0:T(8,128)(2,1)}, bf16[3072,128]{1,0:T(8,128)(2,1)S(1)}, u32[]{:S(2)}, u32[]{:S(2)}) collective-permute-start(bf16[3072,128]{1,0:T(8,128)(2,1)} %collective-permute-done.26.refs_11_), channel_id=1, source_target_pairs={{0,1},{1,0},{2,3},{3,2},{4,5},{5,4},{6,7},{7,6},{8,9},{9,8},{10,11... | collective-permute-start | bytes 2359304 | tf_op jit(solution)/shard_map/ppermute | solution.py:231
  158.0 19.9 %collective-permute-start.23 = (bf16[1024,128]{1,0:T(8,128)(2,1)S(1)}, bf16[1024,128]{1,0:T(8,128)(2,1)S(1)}, u32[]{:S(2)}, u32[]{:S(2)}) collective-permute-start(bf16[1024,128]{1,0:T(8,128)(2,1)S(1)} %slice.18), channel_id=1, source_target_pairs={{0,4},{4,0},{1,5},{5,1},{2,6},{6,2},{3,7},{7,3},{8,12},{12,8},{9,1... | collective-permute-start | bytes 786440 | tf_op jit(solution)/shard_map/ppermute | solution.py:231
  178.0 10.5 %copy-start.8 = (bf16[3072,128]{1,0:T(8,128)(2,1)}, bf16[3072,128]{1,0:T(8,128)(2,1)S(1)}, u32[]{:S(2)}) copy-start(bf16[3072,128]{1,0:T(8,128)(2,1)S(1)} %constant_dynamic-update-slice_fusion.10.refs_11_) | copy-start | bytes 2359300
  178.0 10.5 %collective-permute-start.28 = (bf16[3072,128]{1,0:T(8,128)(2,1)S(1)}, bf16[3072,128]{1,0:T(8,128)(2,1)S(1)}, u32[]{:S(2)}, u32[]{:S(2)}) collective-permute-start(bf16[3072,128]{1,0:T(8,128)(2,1)S(1)} %constant_dynamic-update-slice_fusion.10.refs_11_), channel_id=1, source_target_pairs={{0,1},{1,0},{2,3},{3,2},{4,5},{5,4},{6,7},{7,6},{8,9},{9,8},{10,11... | collective-permute-start | bytes 2359304 | tf_op jit(solution)/shard_map/ppermute | solution.py:231
  178.2 1.0 copy-start.9
  188.5 0.9 copy-start.11
  (3 other events, 2.6 us)
where the time goes:
time: 200 us; the launch traced here: 199 us
  Pallas kernels  78.4 us (39%)
  waiting for transfers between devices  53 us (26%)
  starting transfers between devices  38.9 us (19%)
  local copies, waits for them, and re-layouts  22 us (11%)
  other arithmetic  6.03 us (3%)
    ppermute x30, waiting for transfers between devices, exchange(): return lax.ppermute(value, axis, pairs)  53 us
    pallas_call x5, Pallas kernels, outputs(): pl.pallas_call(kernel, grid_spec=pltpu.PrefetchScalarGridSpec(num_scalar_...  48.2 us
    ppermute x30, starting transfers between devices, exchange(): return lax.ppermute(value, axis, pairs)  28.5 us
    pallas_call x3, Pallas kernels, states(): pl.pallas_call(functools.partial(states_kernel, heads, width, group, padd...  22 us
    unnamed x48, local copies, waits for them, and re-layouts  13.7 us
    all_to_all x1, starting transfers between devices, on_device(): lax.all_to_all(to_owners(after(level_weight, totals[0], *cuts).astype(bf1...  5.7 us
    pallas_call x1, Pallas kernels, on_device(): pl.pallas_call(functools.partial(gates_kernel, heads, levels, padded), ou...  5.27 us
    all_to_all x1, starting transfers between devices, on_device(): lax.all_to_all(to_owners(gates), ('z', 'y'), split_axis=0, concat_axis=0,...  4.68 us
  transfers between devices with their start and end apart: 32, of which 9 were waited for; matrix products, arithmetic and copies ran while one was open for 11% of the time, Pallas kernels for 35%

commit v1 on v0

--- a/solution.py
+++ b/solution.py
@@ -252,18 +252,15 @@
     return near
 
 
-def diagonal(near, by_x, by_y, cuts=None):
+def diagonal(near, by_x, by_y):
     far = {}
-    cuts = [] if cuts is None else cuts
     for y, x in places():
         if y and x:
             parts = []
             if by_x is not None:
-                cuts.append(near[0, x][by_x])
-                parts.append(exchange(cuts[-1], "y", y))
+                parts.append(exchange(near[0, x][by_x], "y", y))
             if by_y is not None:
-                cuts.append(near[y, 0][by_y])
-                parts.append(exchange(cuts[-1], "x", x))
+                parts.append(exchange(near[y, 0][by_y], "x", x))
             far[y, x] = parts
     return far
 
@@ -320,6 +317,7 @@
     )
     gates = lax.all_to_all(to_owners(gates), ("z", "y"), split_axis=0, concat_axis=0, tiled=True)
     query_near = straight(c_proj)
+    query_line = along_z(after(c_proj, *key_line))
     crossed = [near[place] for near in (key_near, query_near) for place in places() if place in near and any(place)]
     everything = slice(None)
     key_near.update({place: join(parts) for place, parts in diagonal(key_near, everything, None).items()})
@@ -450,7 +448,7 @@
     sides = [place for place in places() if (place[0] > 0) != (place[1] > 0)]
     corners = [place for place in places() if place[0] and place[1]]
     far_ids = {place: group_ids(place) for place in places()}
-    lows, cuts = {}, []
+    lows = {}
     if key_line:
         cut = block * ((len(key_line) + 1) // 3)
         by_x, by_y = slice(0, cut), slice(cut, None)
@@ -458,10 +456,9 @@
         keys_far = {one: with_core(key_far[one])}
         begun = [key_far[one]]
         low_here, lows[one] = states([(here, keys_here), (far_ids[one], keys_far[one])])
-        query_line = along_z(after(c_proj, weight))
         if sides:
             tied = {place: after(key_far[place], totals[0]) for place in sides}
-            parts = diagonal(tied, by_x, by_y, cuts)
+            parts = diagonal(tied, by_x, by_y)
             begun = [tied[place] for place in sides]
             keys_far.update({place: with_core(key_far[place]) for place in sides})
             lows.update(zip(sides, states([(far_ids[place], keys_far[place]) for place in sides])))
@@ -474,7 +471,7 @@
     else:
         (low_here,) = states([(here, keys_here)])
     level_rows = lax.all_to_all(
-        to_owners(after(level_weight, totals[0], *cuts).astype(bf16)), ("z", "y"), split_axis=0, concat_axis=0, tiled=True
+        to_owners(after(level_weight, *totals[:2]).astype(bf16)), ("z", "y"), split_axis=0, concat_axis=0, tiled=True
     )
     queries_here = with_core(join([after(query_near[place], totals[0]) for place in places()]))
 

time: 200 us -> 215 us (1.075)
  waiting for transfers between devices: 53 us -> 79.2 us
  local copies, waits for them, and re-layouts: 22 us -> 14.4 us
    all_to_all x1, waiting for transfers between devices: 0.01 us -> 16.7 us  [on_device(): lax.all_to_all(to_owners(gates), ('z', 'y'), split_axis=0, concat_axis=0,...]
    ppermute x30, waiting for transfers between devices: 53 us -> 62.5 us  [exchange(): return lax.ppermute(value, axis, pairs)]
    unnamed x48 -> x64, local copies, waits for them, and re-layouts: 13.7 us -> 7.11 us
  transfers between devices with their start and end apart: 32 -> 32, of which waited for: 9 -> 11; matrix products, arithmetic and copies ran while one was open for 11% -> 7% of each run, Pallas kernels for 35% -> 32%
where the time goes in v1:
time: 215 us; the launch traced here: 214 us
  waiting for transfers between devices  79.2 us (37%)
  Pallas kernels  78.5 us (37%)
  starting transfers between devices  37.2 us (17%)
  local copies, waits for them, and re-layouts  14.4 us (7%)
  other arithmetic  4.26 us (2%)
    ppermute x30, waiting for transfers between devices, exchange(): return lax.ppermute(value, axis, pairs)  62.5 us
    pallas_call x5, Pallas kernels, outputs(): pl.pallas_call(kernel, grid_spec=pltpu.PrefetchScalarGridSpec(num_scalar_...  48.2 us
    ppermute x30, starting transfers between devices, exchange(): return lax.ppermute(value, axis, pairs)  27.8 us
    pallas_call x3, Pallas kernels, states(): pl.pallas_call(functools.partial(states_kernel, heads, width, group, padd...  22.1 us
    all_to_all x1, waiting for transfers between devices, on_device(): lax.all_to_all(to_owners(gates), ('z', 'y'), split_axis=0, concat_axis=0,...  16.7 us
    unnamed x64, local copies, waits for them, and re-layouts  7.11 us
    all_to_all x1, starting transfers between devices, on_device(): lax.all_to_all(to_owners(gates), ('z', 'y'), split_axis=0, concat_axis=0,...  5.54 us
    pallas_call x1, Pallas kernels, on_device(): pl.pallas_call(functools.partial(gates_kernel, heads, levels, padded), ou...  5.27 us
  transfers between devices with their start and end apart: 32, of which 11 were waited for; matrix products, arithmetic and copies ran while one was open for 7% of the time, Pallas kernels for 32%

profile of v1, /device:TPU:0, one launch (start us, length us, event | category | flops | bytes accessed | tf_op | source)
XLA Modules:
  0.0 214.0 jit_solution(17042916907098899829)
XLA Ops:
  0.0 4.0 %collective-permute-start.5 = (bf16[1024,128]{1,0:T(8,128)(2,1)}, bf16[1024,128]{1,0:T(8,128)(2,1)S(1)}, u32[]{:S(2)}, u32[]{:S(2)}) collective-permute-start(bf16[1024,128]{1,0:T(8,128)(2,1)} %param.8), channel_id=1, source_target_pairs={{0,16},{8,24},{16,0},{24,8},{1,17},{9,25},{17,1},{25,9},{2,18},{10... | collective-permute-start | bytes 786440 | tf_op jit(solution)/shard_map/ppermute | solution.py:231
  4.0 1.6 collective-permute-start.4
  5.6 10.7 %collective-permute-done.5 = bf16[1024,128]{1,0:T(8,128)(2,1)S(1)} collective-permute-done((bf16[1024,128]{1,0:T(8,128)(2,1)}, bf16[1024,128]{1,0:T(8,128)(2,1)S(1)}, u32[]{:S(2)}, u32[]{:S(2)}) %collective-permute-start.5) | collective-permute-done | bytes 262176 | tf_op jit(solution)/shard_map/ppermute | solution.py:231
  17.0 1.5 collective-permute-start
  18.5 1.5 collective-permute-start.1
  21.1 2.7 %collective-permute-done.6 = bf16[1024,128]{1,0:T(8,128)(2,1)S(1)} collective-permute-done((bf16[1024,128]{1,0:T(8,128)(2,1)S(1)}, bf16[1024,128]{1,0:T(8,128)(2,1)S(1)}, u32[]{:S(2)}, u32[]{:S(2)}) %collective-permute-start.6) | collective-permute-done | bytes 262176 | tf_op jit(solution)/shard_map/ppermute | solution.py:231
  23.9 2.6 %collective-permute-done = bf16[1024,128]{1,0:T(8,128)(2,1)S(1)} collective-permute-done((bf16[1024,128]{1,0:T(8,128)(2,1)}, bf16[1024,128]{1,0:T(8,128)(2,1)S(1)}, u32[]{:S(2)}, u32[]{:S(2)}) %collective-permute-start) | collective-permute-done | bytes 262176 | tf_op jit(solution)/shard_map/ppermute | solution.py:231
  26.4 5.6 %collective-permute-done.8 = bf16[1024,128]{1,0:T(8,128)(2,1)S(1)} collective-permute-done((bf16[1024,128]{1,0:T(8,128)(2,1)}, bf16[1024,128]{1,0:T(8,128)(2,1)S(1)}, u32[]{:S(2)}, u32[]{:S(2)}) %collective-permute-start.8) | collective-permute-done | bytes 262176 | tf_op jit(solution)/shard_map/ppermute | solution.py:231
  32.6 1.5 collective-permute-start.12
  34.8 21.2 %collective-permute-done.2 = bf16[1024,128]{1,0:T(8,128)(2,1)S(1)} collective-permute-done((bf16[1024,128]{1,0:T(8,128)(2,1)S(1)}, bf16[1024,128]{1,0:T(8,128)(2,1)S(1)}, u32[]{:S(2)}, u32[]{:S(2)}) %collective-permute-start.2) | collective-permute-done | bytes 262176 | tf_op jit(solution)/shard_map/ppermute | solution.py:231
  56.3 0.9 pad_maximum_fusion.2
  57.2 5.5 %all-to-all-start = ((f32[8,4,16,256]{3,2,1,0:T(8,128)}), f32[8,4,16,256]{3,2,1,0:T(8,128)}, u32[]{:S(2)}, u32[]{:S(2)}) async-start(f32[8,4,16,256]{3,2,1,0:T(8,128)} %bitcast.40), calls=%async_computation | async-start | bytes 1048576 | tf_op jit(solution)/shard_map/all_to_all | solution.py:318
  63.5 2.9 %collective-permute-start.18 = (bf16[1024,128]{1,0:T(8,128)(2,1)}, bf16[1024,128]{1,0:T(8,128)(2,1)}, u32[]{:S(2)}, u32[]{:S(2)}) collective-permute-start(bf16[1024,128]{1,0:T(8,128)(2,1)} %param.9), channel_id=1, source_target_pairs={{0,16},{8,24},{16,0},{24,8},{1,17},{9,25},{17,1},{25,9},{2,18},{10... | collective-permute-start | bytes 786440 | tf_op jit(solution)/shard_map/ppermute | solution.py:231
  67.6 16.7 %all-to-all-done.gates_ref = f32[8,4,16,256]{3,2,1,0:T(8,128)} async-done(((f32[8,4,16,256]{3,2,1,0:T(8,128)}), f32[8,4,16,256]{3,2,1,0:T(8,128)}, u32[]{:S(2)}, u32[]{:S(2)}) %all-to-all-start) | async-done | bytes 524320 | tf_op jit(solution)/shard_map/all_to_all | solution.py:318
  84.3 5.3 %gates.1 = (f32[2,128,256]{2,1,0:T(8,128)}, f32[2,128,256]{2,1,0:T(8,128)}, f32[2,128,256]{2,1,0:T(8,128)}, f32[2,128,128]{2,1,0:T(8,128)}, f32[2,1024,128]{2,1,0:T(8,128)}, /*index=5*/f32[2,1024,128]{2,1,0:T(8,128)}) custom-call(f32[8,4,16,256]{3,2,1,0:T(8,128)} %all-to-all-done.gates_ref), custom_call_target="tpu_custom_call" | custom-call | tf_op jit(solution)/shard_map/gates/pallas_call | solution.py:328
  89.6 9.0 %states.3 = (bf16[7,16,128,128]{3,2,1,0:T(8,128)(2,1)}, f32[7,128,128]{2,1,0:T(8,128)}) custom-call(s32[7]{0:T(128)} %concatenate.33.groups_ref, s32[1]{0:T(128)} %bitcast.core_ref.refs_1_, bf16[128,32768]{1,0:T(8,128)(2,1)} %refs_3_.9, f32[2,16,8,256]{3,2,1,0:T(8,128)} %bitcast.37, f32[2,16,8,128]{3,2,1,0:T(8,128)} %bitcast.41, ...), custom_call_target="tpu_custom_call" | custom-call | flops 469762048 | bytes 14680064 | tf_op jit(solution)/shard_map/states/pallas_call | solution.py:362
  98.6 8.0 %states.4 = (bf16[6,16,128,128]{3,2,1,0:T(8,128)(2,1)}, f32[6,128,128]{2,1,0:T(8,128)}) custom-call(s32[6]{0:T(128)} %pad_add_fusion.groups_ref, s32[1]{0:T(128)} %bitcast.core_ref.refs_1_, bf16[128,32768]{1,0:T(8,128)(2,1)} %refs_3_.9, f32[2,16,8,256]{3,2,1,0:T(8,128)} %bitcast.38, f32[2,16,8,128]{3,2,1,0:T(8,128)} %bitcast.42, ...), custom_call_target="tpu_custom_call" | custom-call | flops 402653184 | bytes 12582912 | tf_op jit(solution)/shard_map/states/pallas_call | solution.py:362
  106.7 1.1 convert_element_type.3
  107.8 3.9 %all-to-all-start.1 = ((bf16[8,16,4096]{2,1,0:T(8,128)(2,1)}), bf16[8,16,4096]{2,1,0:T(8,128)(2,1)S(1)}, u32[]{:S(2)}, u32[]{:S(2)}) async-start(bf16[8,16,4096]{2,1,0:T(8,128)(2,1)} %bitcast.14), calls=%async_computation.1 | async-start | bytes 2097152 | tf_op jit(solution)/shard_map/all_to_all | solution.py:473
  111.7 1.6 collective-permute-start.21
  113.2 1.7 collective-permute-start.17
  116.6 1.0 slice.16
  117.6 1.8 collective-permute-start.14
  120.1 0.9 collective-permute-done.21
  121.0 0.7 constant_dynamic-update-slice_fusion.7
  121.7 0.7 constant_dynamic-update-slice_fusion.6.refs_11_
  122.5 6.7 %collective-permute-done.14 = bf16[1024,128]{1,0:T(8,128)(2,1)S(1)} collective-permute-done((bf16[1024,128]{1,0:T(8,128)(2,1)S(1)}, bf16[1024,128]{1,0:T(8,128)(2,1)S(1)}, u32[]{:S(2)}, u32[]{:S(2)}) %collective-permute-start.14) | collective-permute-done | bytes 262176 | tf_op jit(solution)/shard_map/ppermute | solution.py:231
  129.2 0.8 collective-permute-done.15
  130.2 7.5 %collective-permute-done.17 = bf16[1024,128]{1,0:T(8,128)(2,1)S(1)} collective-permute-done((bf16[1024,128]{1,0:T(8,128)(2,1)S(1)}, bf16[1024,128]{1,0:T(8,128)(2,1)S(1)}, u32[]{:S(2)}, u32[]{:S(2)}) %collective-permute-start.17) | collective-permute-done | bytes 262176 | tf_op jit(solution)/shard_map/ppermute | solution.py:231
  137.7 3.8 %collective-permute-done.19 = bf16[1024,128]{1,0:T(8,128)(2,1)S(1)} collective-permute-done((bf16[1024,128]{1,0:T(8,128)(2,1)}, bf16[1024,128]{1,0:T(8,128)(2,1)S(1)}, u32[]{:S(2)}, u32[]{:S(2)}) %collective-permute-start.19) | collective-permute-done | bytes 262176 | tf_op jit(solution)/shard_map/ppermute | solution.py:231
  141.5 1.0 pad_maximum_fusion.1.refs_11_
  142.5 1.6 collective-permute-start.20
  145.8 1.4 collective-permute-start.26
  147.2 1.6 slice_bitcast_fusion.merge_ref
  148.8 0.9 copy-done.8
  149.7 5.1 %states.5 = (bf16[3,16,128,128]{3,2,1,0:T(8,128)(2,1)}, f32[3,128,128]{2,1,0:T(8,128)}) custom-call(s32[3]{0:T(128)} %copy-done.22, s32[1]{0:T(128)} %bitcast.core_ref.refs_1_, bf16[128,32768]{1,0:T(8,128)(2,1)} %refs_3_.9, f32[2,16,8,256]{3,2,1,0:T(8,128)} %bitcast.39, f32[2,16,8,128]{3,2,1,0:T(8,128)} %bitcast.43, ...), custom_call_target="tpu_custom_call" | custom-call | flops 201326592 | bytes 6291456 | tf_op jit(solution)/shard_map/states/pallas_call | solution.py:362
  154.8 2.9 %tree.1.refs_4_ = bf16[16,128,128]{2,1,0:T(8,128)(2,1)} custom-call(s32[16]{0:T(128)} %concatenate.32.groups_ref, f32[2,128,128]{2,1,0:T(8,128)} %slice_bitcast_fusion.merge_ref, f32[7,128,128]{2,1,0:T(8,128)} %get-tuple-element.38.refs_0_, f32[6,128,128]{2,1,0:T(8,128)} %get-tuple-element.39.refs_1_, f32[3,128,128]{2,1,0:T(8,128)} %get-tuple-element.44.refs_2_), custom_call_target="tpu_custom_call" | custom-call | tf_op jit(solution)/shard_map/tree/pallas_call | solution.py:478
  157.7 1.0 copy-done
  158.7 11.3 %outputs.5.refs_14_ = bf16[128,32768]{1,0:T(8,128)(2,1)} custom-call(s32[4]{0:T(128)} %pad_add_fusion.1.refs_0_, s32[1]{0:T(128)} %bitcast.core_ref.refs_1_, f32[2]{0:T(128)} %dynamic_slice.3.refs_2_, bf16[128,32768]{1,0:T(8,128)(2,1)} %refs_3_.9, bf16[16,128,128]{2,1,0:T(8,128)(2,1)} %tree.1.refs_4_, f32[2,16,8,256]{3,2,1,0:T(8,128)} %bitcast.27, ...), custom_call_target="tpu_custom_call" | custom-call | flops 2952790016 | bytes 8388608 | tf_op jit(solution)/shard_map/outputs/pallas_call | solution.py:419
  170.5 1.1 slice.19
  172.2 1.0 slice.18
  173.9 9.3 %outputs.6.refs_14_ = bf16[128,32768]{1,0:T(8,128)(2,1)} custom-call(s32[3]{0:T(128)} %copy-done.23, s32[1]{0:T(128)} %bitcast.core_ref.refs_1_, f32[2]{0:T(128)} %dynamic_slice.3.refs_2_, bf16[128,32768]{1,0:T(8,128)(2,1)} %refs_3_.9, bf16[16,128,128]{2,1,0:T(8,128)(2,1)} %tree.1.refs_4_, ...), custom_call_target="tpu_custom_call", output_to_operand_aliasing={{}: (14, {})} | custom-call | flops 2214592512 | bytes 6291456 | tf_op jit(solution)/shard_map/outputs/pallas_call | solution.py:419
  183.2 0.9 copy-done.12
  184.1 9.2 %outputs.7.refs_14_ = bf16[128,32768]{1,0:T(8,128)(2,1)} custom-call(s32[3]{0:T(128)} %copy-done.25, s32[1]{0:T(128)} %bitcast.core_ref.refs_1_, f32[2]{0:T(128)} %dynamic_slice.3.refs_2_, bf16[128,32768]{1,0:T(8,128)(2,1)} %refs_3_.9, bf16[16,128,128]{2,1,0:T(8,128)(2,1)} %tree.1.refs_4_, ...), custom_call_target="tpu_custom_call", output_to_operand_aliasing={{}: (14, {})} | custom-call | flops 2214592512 | bytes 6291456 | tf_op jit(solution)/shard_map/outputs/pallas_call | solution.py:419
  193.7 0.9 copy-done.11
  194.6 9.3 %outputs.8.refs_14_ = bf16[128,32768]{1,0:T(8,128)(2,1)} custom-call(s32[3]{0:T(128)} %copy-done.24, s32[1]{0:T(128)} %bitcast.core_ref.refs_1_, f32[2]{0:T(128)} %dynamic_slice.3.refs_2_, bf16[128,32768]{1,0:T(8,128)(2,1)} %refs_3_.9, bf16[16,128,128]{2,1,0:T(8,128)(2,1)} %tree.1.refs_4_, ...), custom_call_target="tpu_custom_call", output_to_operand_aliasing={{}: (14, {})} | custom-call | flops 2214592512 | bytes 6291456 | tf_op jit(solution)/shard_map/outputs/pallas_call | solution.py:419
  203.9 0.9 copy-done.13
  204.8 9.2 %outputs.9 = bf16[128,32768]{1,0:T(8,128)(2,1)} custom-call(s32[3]{0:T(128)} %copy-done.22, s32[1]{0:T(128)} %bitcast.core_ref.refs_1_, f32[2]{0:T(128)} %dynamic_slice.3.refs_2_, bf16[128,32768]{1,0:T(8,128)(2,1)} %refs_3_.9, bf16[16,128,128]{2,1,0:T(8,128)(2,1)} %tree.1.refs_4_, f32[2,16,8,256]{3,2,1,0:T(8,128)} %bitcast.31, ...), custom_call_target="tpu_custom_call", output_to_operand_aliasing={{}: (14, {})} | custom-call | flops 2214592512 | bytes 6291456 | tf_op jit(solution)/shard_map/outputs/pallas_call | solution.py:419
  (111 shorter events, 11.9 us)
Async XLA Ops:
  0.0 34.6 %copy-start.14 = (bf16[1024,128]{1,0:T(8,128)(2,1)S(1)}, bf16[1024,128]{1,0:T(8,128)(2,1)}, u32[]{:S(2)}) copy-start(bf16[1024,128]{1,0:T(8,128)(2,1)} %param.8) | copy-start | bytes 786436
  0.0 56.1 %copy-start.15 = (f32[16,4096]{1,0:T(8,128)S(1)}, f32[16,4096]{1,0:T(8,128)}, u32[]{:S(2)}) copy-start(f32[16,4096]{1,0:T(8,128)} %param.10) | copy-start | bytes 786436
  0.0 16.3 %collective-permute-start.5 = (bf16[1024,128]{1,0:T(8,128)(2,1)}, bf16[1024,128]{1,0:T(8,128)(2,1)S(1)}, u32[]{:S(2)}, u32[]{:S(2)}) collective-permute-start(bf16[1024,128]{1,0:T(8,128)(2,1)} %param.8), channel_id=1, source_target_pairs={{0,16},{8,24},{16,0},{24,8},{1,17},{9,25},{17,1},{25,9},{2,18},{10... | collective-permute-start | bytes 786440 | tf_op jit(solution)/shard_map/ppermute | solution.py:231
  4.0 16.5 %collective-permute-start.4 = (bf16[1024,128]{1,0:T(8,128)(2,1)}, bf16[1024,128]{1,0:T(8,128)(2,1)S(1)}, u32[]{:S(2)}, u32[]{:S(2)}) collective-permute-start(bf16[1024,128]{1,0:T(8,128)(2,1)} %param.8), channel_id=1, source_target_pairs={{0,8},{8,0},{16,24},{24,16},{1,9},{9,1},{17,25},{25,17},{2,10},{10... | collective-permute-start | bytes 786440 | tf_op jit(solution)/shard_map/ppermute | solution.py:231
  16.3 7.4 %collective-permute-start.6 = (bf16[1024,128]{1,0:T(8,128)(2,1)S(1)}, bf16[1024,128]{1,0:T(8,128)(2,1)S(1)}, u32[]{:S(2)}, u32[]{:S(2)}) collective-permute-start(bf16[1024,128]{1,0:T(8,128)(2,1)S(1)} %collective-permute-done.5), channel_id=1, source_target_pairs={{0,8},{8,0},{16,24},{24,16},{1,9},{9,1},{17,25},{25,17},{2,10},{10... | collective-permute-start | bytes 786440 | tf_op jit(solution)/shard_map/ppermute | solution.py:231
  17.0 9.4 %collective-permute-start = (bf16[1024,128]{1,0:T(8,128)(2,1)}, bf16[1024,128]{1,0:T(8,128)(2,1)S(1)}, u32[]{:S(2)}, u32[]{:S(2)}) collective-permute-start(bf16[1024,128]{1,0:T(8,128)(2,1)} %param.8), channel_id=1, source_target_pairs={{0,2},{2,0},{1,3},{3,1},{4,6},{6,4},{5,7},{7,5},{8,10},{10,8},{9,1... | collective-permute-start | bytes 786440 | tf_op jit(solution)/shard_map/ppermute | solution.py:231
  18.5 13.5 %collective-permute-start.1 = (bf16[1024,128]{1,0:T(8,128)(2,1)}, bf16[1024,128]{1,0:T(8,128)(2,1)S(1)}, u32[]{:S(2)}, u32[]{:S(2)}) collective-permute-start(bf16[1024,128]{1,0:T(8,128)(2,1)} %param.8), channel_id=1, source_target_pairs={{0,4},{4,0},{1,5},{5,1},{2,6},{6,2},{3,7},{7,3},{8,12},{12,8},{9,1... | collective-permute-start | bytes 786440 | tf_op jit(solution)/shard_map/ppermute | solution.py:231
  20.0 12.0 %collective-permute-start.8 = (bf16[1024,128]{1,0:T(8,128)(2,1)}, bf16[1024,128]{1,0:T(8,128)(2,1)S(1)}, u32[]{:S(2)}, u32[]{:S(2)}) collective-permute-start(bf16[1024,128]{1,0:T(8,128)(2,1)} %param.9), channel_id=1, source_target_pairs={{0,4},{4,0},{1,5},{5,1},{2,6},{6,2},{3,7},{7,3},{8,12},{12,8},{9,1... | collective-permute-start | bytes 786440 | tf_op jit(solution)/shard_map/ppermute | solution.py:231
  20.5 11.5 %collective-permute-start.7 = (bf16[1024,128]{1,0:T(8,128)(2,1)}, bf16[1024,128]{1,0:T(8,128)(2,1)S(1)}, u32[]{:S(2)}, u32[]{:S(2)}) collective-permute-start(bf16[1024,128]{1,0:T(8,128)(2,1)} %param.9), channel_id=1, source_target_pairs={{0,2},{2,0},{1,3},{3,1},{4,6},{6,4},{5,7},{7,5},{8,10},{10,8},{9,1... | collective-permute-start | bytes 786440 | tf_op jit(solution)/shard_map/ppermute | solution.py:231
  23.8 38.9 %copy-start.1 = (bf16[3072,128]{1,0:T(8,128)(2,1)}, bf16[3072,128]{1,0:T(8,128)(2,1)S(1)}, u32[]{:S(2)}) copy-start(bf16[3072,128]{1,0:T(8,128)(2,1)S(1)} %pad_maximum_fusion.refs_2_.refs_9_) | copy-start | bytes 2359300
  23.8 32.3 %copy-start.16 = (f32[16,4096]{1,0:T(8,128)S(1)}, f32[16,4096]{1,0:T(8,128)}, u32[]{:S(2)}) copy-start(f32[16,4096]{1,0:T(8,128)} %param.11) | copy-start | bytes 786436
  32.0 24.3 %copy-start.18 = (bf16[1024,128]{1,0:T(8,128)(2,1)}, bf16[1024,128]{1,0:T(8,128)(2,1)S(1)}, u32[]{:S(2)}) copy-start(bf16[1024,128]{1,0:T(8,128)(2,1)S(1)} %collective-permute-done.8) | copy-start | bytes 786436
  32.0 24.3 %copy-start.20 = (bf16[1024,128]{1,0:T(8,128)(2,1)}, bf16[1024,128]{1,0:T(8,128)(2,1)S(1)}, u32[]{:S(2)}) copy-start(bf16[1024,128]{1,0:T(8,128)(2,1)S(1)} %collective-permute-done.7) | copy-start | bytes 786436
  32.0 30.9 %collective-permute-start.10 = (bf16[3072,128]{1,0:T(8,128)(2,1)S(1)}, bf16[3072,128]{1,0:T(8,128)(2,1)S(1)}, u32[]{:S(2)}, u32[]{:S(2)}) collective-permute-start(bf16[3072,128]{1,0:T(8,128)(2,1)S(1)} %pad_maximum_fusion.refs_2_.refs_9_), channel_id=1, source_target_pairs={{0,2},{2,0},{1,3},{3,1},{4,6},{6,4},{5,7},{7,5},{8,10},{10,8},{9,1... | collective-permute-start | bytes 2359304 | tf_op jit(solution)/shard_map/ppermute | solution.py:231
  32.6 30.7 %collective-permute-start.12 = (bf16[3072,128]{1,0:T(8,128)(2,1)S(1)}, bf16[3072,128]{1,0:T(8,128)(2,1)S(1)}, u32[]{:S(2)}, u32[]{:S(2)}) collective-permute-start(bf16[3072,128]{1,0:T(8,128)(2,1)S(1)} %pad_maximum_fusion.refs_2_.refs_9_), channel_id=1, source_target_pairs={{0,4},{4,0},{1,5},{5,1},{2,6},{6,2},{3,7},{7,3},{8,12},{12,8},{9,1... | collective-permute-start | bytes 2359304 | tf_op jit(solution)/shard_map/ppermute | solution.py:231
  34.1 21.8 %collective-permute-start.2 = (bf16[1024,128]{1,0:T(8,128)(2,1)S(1)}, bf16[1024,128]{1,0:T(8,128)(2,1)S(1)}, u32[]{:S(2)}, u32[]{:S(2)}) collective-permute-start(bf16[1024,128]{1,0:T(8,128)(2,1)S(1)} %collective-permute-done), channel_id=1, source_target_pairs={{0,4},{4,0},{1,5},{5,1},{2,6},{6,2},{3,7},{7,3},{8,12},{12,8},{9,1... | collective-permute-start | bytes 786440 | tf_op jit(solution)/shard_map/ppermute | solution.py:231
  56.0 33.6 %collective-permute-start.3 = (bf16[4096,128]{1,0:T(8,128)(2,1)S(1)}, bf16[4096,128]{1,0:T(8,128)(2,1)}, u32[]{:S(2)}, u32[]{:S(2)}) collective-permute-start(bf16[4096,128]{1,0:T(8,128)(2,1)S(1)} %constant_dynamic-update-slice_fusion.refs_0_.refs_9_), channel_id=1, source_target_pairs={{0,1},{1,0},{2,3},{3,2},{4,5},{5,4},{6,7},{7,6},{8,9},{9,8},{10,11... | collective-permute-start | bytes 3145736 | tf_op jit(solution)/shard_map/ppermute | solution.py:231
  57.2 27.1 %all-to-all-start = ((f32[8,4,16,256]{3,2,1,0:T(8,128)}), f32[8,4,16,256]{3,2,1,0:T(8,128)}, u32[]{:S(2)}, u32[]{:S(2)}) async-start(f32[8,4,16,256]{3,2,1,0:T(8,128)} %bitcast.40), calls=%async_computation | async-start | bytes 1048576 | tf_op jit(solution)/shard_map/all_to_all | solution.py:318
  62.7 26.9 %collective-permute-start.9 = (bf16[3072,128]{1,0:T(8,128)(2,1)S(1)}, bf16[3072,128]{1,0:T(8,128)(2,1)}, u32[]{:S(2)}, u32[]{:S(2)}) collective-permute-start(bf16[3072,128]{1,0:T(8,128)(2,1)S(1)} %pad_maximum_fusion.refs_2_.refs_9_), channel_id=1, source_target_pairs={{0,1},{1,0},{2,3},{3,2},{4,5},{5,4},{6,7},{7,6},{8,9},{9,8},{10,11... | collective-permute-start | bytes 2359304 | tf_op jit(solution)/shard_map/ppermute | solution.py:231
  62.9 35.6 %copy-start.5 = (bf16[3072,128]{1,0:T(8,128)(2,1)}, bf16[3072,128]{1,0:T(8,128)(2,1)S(1)}, u32[]{:S(2)}) copy-start(bf16[3072,128]{1,0:T(8,128)(2,1)S(1)} %collective-permute-done.10.refs_0_.refs_9_) | copy-start | bytes 2359300
  62.9 35.6 %collective-permute-start.11 = (bf16[3072,128]{1,0:T(8,128)(2,1)S(1)}, bf16[3072,128]{1,0:T(8,128)(2,1)}, u32[]{:S(2)}, u32[]{:S(2)}) collective-permute-start(bf16[3072,128]{1,0:T(8,128)(2,1)S(1)} %collective-permute-done.10.refs_0_.refs_9_), channel_id=1, source_target_pairs={{0,1},{1,0},{2,3},{3,2},{4,5},{5,4},{6,7},{7,6},{8,9},{9,8},{10,11... | collective-permute-start | bytes 2359304 | tf_op jit(solution)/shard_map/ppermute | solution.py:231
  63.3 35.3 %copy-start.2 = (bf16[3072,128]{1,0:T(8,128)(2,1)}, bf16[3072,128]{1,0:T(8,128)(2,1)S(1)}, u32[]{:S(2)}) copy-start(bf16[3072,128]{1,0:T(8,128)(2,1)S(1)} %collective-permute-done.12.refs_2_.refs_9_) | copy-start | bytes 2359300
  63.3 35.3 %collective-permute-start.13 = (bf16[3072,128]{1,0:T(8,128)(2,1)S(1)}, bf16[3072,128]{1,0:T(8,128)(2,1)}, u32[]{:S(2)}, u32[]{:S(2)}) collective-permute-start(bf16[3072,128]{1,0:T(8,128)(2,1)S(1)} %collective-permute-done.12.refs_2_.refs_9_), channel_id=1, source_target_pairs={{0,1},{1,0},{2,3},{3,2},{4,5},{5,4},{6,7},{7,6},{8,9},{9,8},{10,11... | collective-permute-start | bytes 2359304 | tf_op jit(solution)/shard_map/ppermute | solution.py:231
  63.5 80.6 %copy-start.25 = (s32[3]{0:T(128)}, s32[3]{0:T(128)S(1)}, u32[]{:S(2)}) copy-start(s32[3]{0:T(128)S(1)} %broadcast_add_fusion.2.refs_0_) | copy-start | bytes 40
  63.5 80.6 %copy-start.23 = (s32[3]{0:T(128)}, s32[3]{0:T(128)S(1)}, u32[]{:S(2)}) copy-start(s32[3]{0:T(128)S(1)} %get-tuple-element.64.refs_0_) | copy-start | bytes 40
  63.5 80.6 %copy-start.24 = (s32[3]{0:T(128)}, s32[3]{0:T(128)S(1)}, u32[]{:S(2)}) copy-start(s32[3]{0:T(128)S(1)} %get-tuple-element.63.refs_0_) | copy-start | bytes 40
  63.5 51.5 %collective-permute-start.18 = (bf16[1024,128]{1,0:T(8,128)(2,1)}, bf16[1024,128]{1,0:T(8,128)(2,1)}, u32[]{:S(2)}, u32[]{:S(2)}) collective-permute-start(bf16[1024,128]{1,0:T(8,128)(2,1)} %param.9), channel_id=1, source_target_pairs={{0,16},{8,24},{16,0},{24,8},{1,17},{9,25},{17,1},{25,9},{2,18},{10... | collective-permute-start | bytes 786440 | tf_op jit(solution)/shard_map/ppermute | solution.py:231
  98.6 8.1 %copy-start.9 = (f32[16,8,4096]{2,1,0:T(8,128)S(1)}, f32[16,8,4096]{2,1,0:T(8,128)}, u32[]{:S(2)}) copy-start(f32[16,8,4096]{2,1,0:T(8,128)} %param.12) | copy-start | bytes 6291460
  107.8 49.9 %all-to-all-start.1 = ((bf16[8,16,4096]{2,1,0:T(8,128)(2,1)}), bf16[8,16,4096]{2,1,0:T(8,128)(2,1)S(1)}, u32[]{:S(2)}, u32[]{:S(2)}) async-start(bf16[8,16,4096]{2,1,0:T(8,128)(2,1)} %bitcast.14), calls=%async_computation.1 | async-start | bytes 2097152 | tf_op jit(solution)/shard_map/all_to_all | solution.py:473
  111.7 9.3 %collective-permute-start.21 = (bf16[1024,128]{1,0:T(8,128)(2,1)S(1)}, bf16[1024,128]{1,0:T(8,128)(2,1)S(1)}, u32[]{:S(2)}, u32[]{:S(2)}) collective-permute-start(bf16[1024,128]{1,0:T(8,128)(2,1)S(1)} %copy-done.19), channel_id=1, source_target_pairs={{0,2},{2,0},{1,3},{3,1},{4,6},{6,4},{5,7},{7,5},{8,10},{10,8},{9,1... | collective-permute-start | bytes 786440 | tf_op jit(solution)/shard_map/ppermute | solution.py:231
  113.2 24.4 %collective-permute-start.17 = (bf16[1024,128]{1,0:T(8,128)(2,1)S(1)}, bf16[1024,128]{1,0:T(8,128)(2,1)S(1)}, u32[]{:S(2)}, u32[]{:S(2)}) collective-permute-start(bf16[1024,128]{1,0:T(8,128)(2,1)S(1)} %copy-done.17), channel_id=1, source_target_pairs={{0,8},{8,0},{16,24},{24,16},{1,9},{9,1},{17,25},{25,17},{2,10},{10... | collective-permute-start | bytes 786440 | tf_op jit(solution)/shard_map/ppermute | solution.py:231
  115.0 26.5 %collective-permute-start.19 = (bf16[1024,128]{1,0:T(8,128)(2,1)}, bf16[1024,128]{1,0:T(8,128)(2,1)S(1)}, u32[]{:S(2)}, u32[]{:S(2)}) collective-permute-start(bf16[1024,128]{1,0:T(8,128)(2,1)} %collective-permute-done.18), channel_id=1, source_target_pairs={{0,8},{8,0},{16,24},{24,16},{1,9},{9,1},{17,25},{25,17},{2,10},{10... | collective-permute-start | bytes 786440 | tf_op jit(solution)/shard_map/ppermute | solution.py:231
  115.3 14.7 %collective-permute-start.15 = (bf16[2048,128]{1,0:T(8,128)(2,1)S(1)}, bf16[2048,128]{1,0:T(8,128)(2,1)S(1)}, u32[]{:S(2)}, u32[]{:S(2)}) collective-permute-start(bf16[2048,128]{1,0:T(8,128)(2,1)S(1)} %slice.17), channel_id=1, source_target_pairs={{0,2},{2,0},{1,3},{3,1},{4,6},{6,4},{5,7},{7,5},{8,10},{10,8},{9,1... | collective-permute-start | bytes 1572872 | tf_op jit(solution)/shard_map/ppermute | solution.py:231
  117.6 11.6 %collective-permute-start.14 = (bf16[1024,128]{1,0:T(8,128)(2,1)S(1)}, bf16[1024,128]{1,0:T(8,128)(2,1)S(1)}, u32[]{:S(2)}, u32[]{:S(2)}) collective-permute-start(bf16[1024,128]{1,0:T(8,128)(2,1)S(1)} %slice.16), channel_id=1, source_target_pairs={{0,4},{4,0},{1,5},{5,1},{2,6},{6,2},{3,7},{7,3},{8,12},{12,8},{9,1... | collective-permute-start | bytes 786440 | tf_op jit(solution)/shard_map/ppermute | solution.py:231
  122.5 22.2 %copy-start.26 = (f32[16]{0:T(128)S(1)}, f32[16]{0:T(128)}, u32[]{:S(2)}) copy-start(f32[16]{0:T(128)} %param.13) | copy-start | bytes 196
  122.5 35.2 %collective-permute-start.22 = (bf16[4096,128]{1,0:T(8,128)(2,1)}, bf16[4096,128]{1,0:T(8,128)(2,1)}, u32[]{:S(2)}, u32[]{:S(2)}) collective-permute-start(bf16[4096,128]{1,0:T(8,128)(2,1)} %constant_dynamic-update-slice_fusion.6.refs_11_), channel_id=1, source_target_pairs={{0,1},{1,0},{2,3},{3,2},{4,5},{5,4},{6,7},{7,6},{8,9},{9,8},{10,11... | collective-permute-start | bytes 3145736 | tf_op jit(solution)/shard_map/ppermute | solution.py:231
  130.1 18.7 %copy-start.6 = (bf16[3072,128]{1,0:T(8,128)(2,1)}, bf16[3072,128]{1,0:T(8,128)(2,1)S(1)}, u32[]{:S(2)}) copy-start(bf16[3072,128]{1,0:T(8,128)(2,1)S(1)} %constant_dynamic-update-slice_fusion.4.refs_0_.refs_9_) | copy-start | bytes 2359300
  130.1 18.7 %collective-permute-start.16 = (bf16[3072,128]{1,0:T(8,128)(2,1)S(1)}, bf16[3072,128]{1,0:T(8,128)(2,1)S(1)}, u32[]{:S(2)}, u32[]{:S(2)}) collective-permute-start(bf16[3072,128]{1,0:T(8,128)(2,1)S(1)} %constant_dynamic-update-slice_fusion.4.refs_0_.refs_9_), channel_id=1, source_target_pairs={{0,1},{1,0},{2,3},{3,2},{4,5},{5,4},{6,7},{7,6},{8,9},{9,8},{10,11... | collective-permute-start | bytes 2359304 | tf_op jit(solution)/shard_map/ppermute | solution.py:231
  142.5 12.3 %copy-start.7 = (bf16[3072,128]{1,0:T(8,128)(2,1)}, bf16[3072,128]{1,0:T(8,128)(2,1)S(1)}, u32[]{:S(2)}) copy-start(bf16[3072,128]{1,0:T(8,128)(2,1)S(1)} %pad_maximum_fusion.1.refs_11_) | copy-start | bytes 2359300
  142.5 27.5 %collective-permute-start.20 = (bf16[3072,128]{1,0:T(8,128)(2,1)S(1)}, bf16[3072,128]{1,0:T(8,128)(2,1)}, u32[]{:S(2)}, u32[]{:S(2)}) collective-permute-start(bf16[3072,128]{1,0:T(8,128)(2,1)S(1)} %pad_maximum_fusion.1.refs_11_), channel_id=1, source_target_pairs={{0,2},{2,0},{1,3},{3,1},{4,6},{6,4},{5,7},{7,5},{8,10},{10,8},{9,1... | collective-permute-start | bytes 2359304 | tf_op jit(solution)/shard_map/ppermute | solution.py:231
  145.8 24.7 %collective-permute-start.26 = (bf16[3072,128]{1,0:T(8,128)(2,1)S(1)}, bf16[3072,128]{1,0:T(8,128)(2,1)}, u32[]{:S(2)}, u32[]{:S(2)}) collective-permute-start(bf16[3072,128]{1,0:T(8,128)(2,1)S(1)} %pad_maximum_fusion.1.refs_11_), channel_id=1, source_target_pairs={{0,4},{4,0},{1,5},{5,1},{2,6},{6,2},{3,7},{7,3},{8,12},{12,8},{9,1... | collective-permute-start | bytes 2359304 | tf_op jit(solution)/shard_map/ppermute | solution.py:231
  148.8 25.1 %collective-permute-start.25 = (bf16[3072,128]{1,0:T(8,128)(2,1)S(1)}, bf16[3072,128]{1,0:T(8,128)(2,1)}, u32[]{:S(2)}, u32[]{:S(2)}) collective-permute-start(bf16[3072,128]{1,0:T(8,128)(2,1)S(1)} %pad_maximum_fusion.1.refs_11_), channel_id=1, source_target_pairs={{0,1},{1,0},{2,3},{3,2},{4,5},{5,4},{6,7},{7,6},{8,9},{9,8},{10,11... | collective-permute-start | bytes 2359304 | tf_op jit(solution)/shard_map/ppermute | solution.py:231
  170.0 13.2 %collective-permute-start.24 = (bf16[3072,128]{1,0:T(8,128)(2,1)}, bf16[3072,128]{1,0:T(8,128)(2,1)S(1)}, u32[]{:S(2)}, u32[]{:S(2)}) collective-permute-start(bf16[3072,128]{1,0:T(8,128)(2,1)} %collective-permute-done.20.refs_11_), channel_id=1, source_target_pairs={{0,1},{1,0},{2,3},{3,2},{4,5},{5,4},{6,7},{7,6},{8,9},{9,8},{10,11... | collective-permute-start | bytes 2359304 | tf_op jit(solution)/shard_map/ppermute | solution.py:231
  171.6 21.7 %collective-permute-start.27 = (bf16[2048,128]{1,0:T(8,128)(2,1)S(1)}, bf16[2048,128]{1,0:T(8,128)(2,1)S(1)}, u32[]{:S(2)}, u32[]{:S(2)}) collective-permute-start(bf16[2048,128]{1,0:T(8,128)(2,1)S(1)} %slice.19), channel_id=1, source_target_pairs={{0,2},{2,0},{1,3},{3,1},{4,6},{6,4},{5,7},{7,5},{8,10},{10,8},{9,1... | collective-permute-start | bytes 1572872 | tf_op jit(solution)/shard_map/ppermute | solution.py:231
  173.2 20.5 %collective-permute-start.29 = (bf16[3072,128]{1,0:T(8,128)(2,1)}, bf16[3072,128]{1,0:T(8,128)(2,1)S(1)}, u32[]{:S(2)}, u32[]{:S(2)}) collective-permute-start(bf16[3072,128]{1,0:T(8,128)(2,1)} %collective-permute-done.26.refs_11_), channel_id=1, source_target_pairs={{0,1},{1,0},{2,3},{3,2},{4,5},{5,4},{6,7},{7,6},{8,9},{9,8},{10,11... | collective-permute-start | bytes 2359304 | tf_op jit(solution)/shard_map/ppermute | solution.py:231
  173.3 20.0 %collective-permute-start.23 = (bf16[1024,128]{1,0:T(8,128)(2,1)S(1)}, bf16[1024,128]{1,0:T(8,128)(2,1)S(1)}, u32[]{:S(2)}, u32[]{:S(2)}) collective-permute-start(bf16[1024,128]{1,0:T(8,128)(2,1)S(1)} %slice.18), channel_id=1, source_target_pairs={{0,4},{4,0},{1,5},{5,1},{2,6},{6,2},{3,7},{7,3},{8,12},{12,8},{9,1... | collective-permute-start | bytes 786440 | tf_op jit(solution)/shard_map/ppermute | solution.py:231
  193.4 10.4 %copy-start.10 = (bf16[3072,128]{1,0:T(8,128)(2,1)}, bf16[3072,128]{1,0:T(8,128)(2,1)S(1)}, u32[]{:S(2)}) copy-start(bf16[3072,128]{1,0:T(8,128)(2,1)S(1)} %constant_dynamic-update-slice_fusion.10.refs_11_) | copy-start | bytes 2359300
  193.4 10.4 %collective-permute-start.28 = (bf16[3072,128]{1,0:T(8,128)(2,1)S(1)}, bf16[3072,128]{1,0:T(8,128)(2,1)S(1)}, u32[]{:S(2)}, u32[]{:S(2)}) collective-permute-start(bf16[3072,128]{1,0:T(8,128)(2,1)S(1)} %constant_dynamic-update-slice_fusion.10.refs_11_), channel_id=1, source_target_pairs={{0,1},{1,0},{2,3},{3,2},{4,5},{5,4},{6,7},{7,6},{8,9},{9,8},{10,11... | collective-permute-start | bytes 2359304 | tf_op jit(solution)/shard_map/ppermute | solution.py:231
  (11 other events, 35.1 us)
